TPU v7x, 32 devices: a whole 2x2x4 slice. The times are simulated.
32 devices in a mesh: cons: 4 (over y, core), ty: 2 (over x), tx: 4 (over z).
Axes of the slice: x: 2, y: 2, z: 4, core: 2. Of those that a mesh axis runs over, the one named last changes fastest.
Arguments:
- elevation: float32 [8, 2, 288, 2048], P('cons', None, 'ty', 'tx'), may hold values from -6 to 6
- equilibrium: float32 [8, 2, 288, 2048], P('cons', None, 'ty', 'tx'), may hold values from -5 to 5
- depth: float32 [288, 2048], P('ty', 'tx'), may hold values from 0.1 to 1
- land_mask: int32 [288, 2048], P('ty', 'tx'), may hold values 0 or 1
- friction_prev: float32 [288, 2048], P('ty', 'tx'), may hold values from 0.3 to 3
Outputs:
- elevation_out: float32 [8, 2, 288, 2048], P('cons', None, 'ty', 'tx')
- friction: float32 [288, 2048], P('ty', 'tx')
All inputs are finite; a program needn't handle non-finite values. No bound on the sum of `land_mask` on one device may be relied on, other than what follows from the above.
Results may differ from a plain program's by a relative error of at most 0.00002.
Values sent between devices are 32-bit elements; how exact they have to be, the bound alone decides.
No kernel may reach another device: no remote copies, remote signals or barrier semaphores. Data moves between devices by JAX's collectives and lax.ppermute only.
A program may use at most 64 MiB of HBM per device.

v0:
```python
import functools
import math

import jax
import jax.numpy as jnp
from jax import lax
from jax.experimental import pallas as pl
from jax.experimental.pallas import tpu as pltpu
from jax.sharding import PartitionSpec as P

OMEGA_TABLE = (1.0, 1.0351, 0.9582, 1.0379, 0.5181, 0.4816, 0.5164, 0.4454)
AY = 0.5
THETA = 0.05
DRAG = 0.5
BACKGROUND = 0.01
F32 = jnp.float32
LANES = 128
MSG = 16
TINY_DEPTH = 1e-6
PARAMS = pltpu.CompilerParams(vmem_limit_bytes=16 * 1024 * 1024)


def vmem(x):
    return pltpu.with_memory_space_constraint(x, pltpu.VMEM)


def hbm(x):
    return pltpu.with_memory_space_constraint(x, pltpu.HBM)


def recip(x):
    return pl.reciprocal(x, approx=True) if jnp.ndim(x) else 1.0 / x


def metric(rows, total):
    lat = (rows + 0.5) * (120.0 / total * math.pi / 180.0) - math.pi / 3.0
    s = lat * lat
    acc = jnp.full_like(s, 1.0 / math.factorial(16))
    for n in (14, 12, 10, 8, 6, 4, 2, 0):
        acc = ((-1.0) ** (n // 2)) / math.factorial(n) + s * acc
    return 0.5 / acc


def omegas(kdev):
    index = lax.axis_index("cons")
    out = []
    for c in range(kdev):
        w = jnp.float32(OMEGA_TABLE[c])
        for i in range(1, len(OMEGA_TABLE) // kdev):
            w = jnp.where(index == i, jnp.float32(OMEGA_TABLE[i * kdev + c]), w)
        out.append(w)
    return out


def rolled(x, shift, axis):
    return pltpu.roll(x, shift % x.shape[axis], axis)


def face(zr, zi, zr_next, zi_next, r2, coef, w2):
    g = coef * recip(r2 * r2 + w2 * w2)
    a = g * r2
    b = g * w2
    dr = zr - zr_next
    di = zi - zi_next
    return a * dr + b * di, a * di - b * dr


def flux(dr, di, g, a, w2):
    b = g * w2
    return a * dr + b * di, a * di - b * dr


def pack_columns_kernel(e_in, q_in, d_in, m_in, r_in, m2, m1, e, q, d, m, r, turned, behind, sems):
    rows, width = d_in.shape
    copies = []
    for s, side in enumerate((slice(0, LANES), slice(width - LANES, width))):
        for src, dst in ((e_in, e), (q_in, q)):
            copies.append((src.at[:, :, :, side], dst.at[s]))
        for src, dst in ((d_in, d), (m_in, m), (r_in, r)):
            copies.append((src.at[:, side], dst.at[s]))
    copies = [pltpu.make_async_copy(src, dst, sems.at[k]) for k, (src, dst) in enumerate(copies)]
    for copy in copies:
        copy.start()
    for copy in copies:
        copy.wait()
    lane = lax.broadcasted_iota(jnp.int32, (rows, LANES), 1)

    def edges(plane):
        return jnp.where(lane < LANES // 2, plane(0), plane(1))

    elev = [edges(lambda s: e[s, c, p]) for p in range(2) for c in range(2)]
    equil = [edges(lambda s: q[s, c, p]) for p in range(2) for c in range(2)]
    planes = [x - y for x, y in zip(elev, equil)]
    planes += [edges(lambda s: r[s]), edges(lambda s: d[s]), edges(lambda s: m[s]).astype(F32)]
    both = jnp.zeros((rows, LANES), F32)
    for k, plane in enumerate(planes + elev):
        both = jnp.where((lane >= 4 * k) & (lane < 4 * k + 4), rolled(plane, 4 * k + 2, 1), both)
    pad = turned.shape[1]
    turned[...] = jnp.concatenate([both, jnp.zeros((pad - rows, LANES), F32)], axis=0).T
    odd = lax.rem(lax.axis_index("tx"), 2)
    first = (lax.axis_index("ty") * rows).astype(F32)
    lat_row = jnp.minimum(lax.broadcasted_iota(jnp.int32, (8, pad), 1), rows).astype(F32) + first
    ax = metric(lat_row, rows * lax.axis_size("ty"))
    w0, w1 = omegas(2)
    w2 = 2.0 * jnp.where(lax.broadcasted_iota(jnp.int32, (8, pad), 0) < 4, w0, w1)
    up = lambda x: rolled(x, -1, 0)
    zr, zi = turned[0:8, :], turned[8:16, :]
    r8, d8, m8 = (jnp.concatenate([turned[at : at + 4, :]] * 2, axis=0) for at in (16, 20, 24))
    coef = (THETA * ax * ax) * (m8 * up(m8) * (d8 + up(d8)))
    behind[0:8, :], behind[8:16, :] = face(zr, zi, up(zr), up(zi), r8 + up(r8), coef, w2)
    for out, west in ((m1, odd), (m2, 1 - odd)):
        lanes = slice(0, out.shape[1])
        for k in range(4):
            out[k : k + 1, :] = turned[pl.ds(4 * k + 1 + west, 1), lanes]
            out[4 + k : 5 + k, :] = behind[pl.ds(4 * k + 2 * west, 1), lanes]
            out[8 + k : 9 + k, :] = turned[pl.ds(4 * (7 + k) + 1 + west, 1), lanes]
        for k in range(3):
            out[12 + k : 13 + k, :] = turned[pl.ds(4 * (4 + k) + 1 + west, 1), lanes]
        out[MSG - 1 :, :] = jnp.zeros((1, out.shape[1]), F32)


def pack_columns(elevation, equilibrium, depth, land_mask, friction):
    kdev, _, rows, width = elevation.shape
    pad = -(-rows // LANES) * LANES
    cut, plane = pltpu.VMEM((2, kdev, 2, rows, LANES), F32), pltpu.VMEM((2, rows, LANES), F32)
    return pl.pallas_call(
        pack_columns_kernel,
        out_shape=(pltpu.VMEM((MSG, rows), F32), pltpu.VMEM((MSG, pad), F32)),
        in_specs=[pl.BlockSpec(memory_space=pltpu.HBM)] * 5,
        out_specs=[pl.BlockSpec(memory_space=pltpu.VMEM)] * 2,
        scratch_shapes=[
            cut,
            cut,
            plane,
            pltpu.VMEM((2, rows, LANES), jnp.int32),
            plane,
            pltpu.VMEM((LANES, pad), F32),
            pltpu.VMEM((16, pad), F32),
            pltpu.SemaphoreType.DMA((10,)),
        ],
        compiler_params=PARAMS,
        name="pack_columns",
    )(*map(hbm, (elevation, equilibrium, depth, land_mask, friction)))


def pack_kernel(e, q, d, ints, r, after, m, mn, ms):
    del after
    kdev, _, rows, width = e.shape
    m[...] = ints[...].astype(F32)
    ws = omegas(kdev)
    for out, end, near, low in ((ms, slice(0, 8), 0, 0), (mn, slice(rows - 8, rows), 7, 6)):
        out[:, width:] = jnp.zeros((MSG, LANES), F32)
        r8, d8, m8 = r[end, :], d[end, :], m[end, :]
        up = lambda x: rolled(x, -1, 0)
        coef = (THETA * AY * AY) * (m8 * up(m8) * (d8 + up(d8)))
        r2 = r8 + up(r8)
        for c in range(kdev):
            elev = [e[c, p, end, :] for p in range(2)]
            z = [elev[p] - q[c, p, end, :] for p in range(2)]
            v = face(z[0], z[1], up(z[0]), up(z[1]), r2, coef, 2.0 * ws[c])
            for p in range(2):
                out[2 * p + c, :width] = z[p][near, :]
                out[4 + 2 * p + c, :width] = v[p][low, :]
                out[8 + 2 * p + c, :width] = elev[p][near, :]
        for k, plane in enumerate((r8, d8, m8)):
            out[12 + k, :width] = plane[near, :]
        out[MSG - 1, :width] = jnp.zeros((width,), F32)


def pack(elevation, equilibrium, depth, land_mask, friction, after):
    kdev, _, rows, width = elevation.shape
    plane = pltpu.VMEM(depth.shape, F32)
    row = pltpu.VMEM((MSG, width + LANES), F32)
    return pl.pallas_call(
        pack_kernel,
        out_shape=(plane, row, row),
        in_specs=[pl.BlockSpec(memory_space=pltpu.VMEM)] * 6,
        out_specs=[pl.BlockSpec(memory_space=pltpu.VMEM)] * 3,
        compiler_params=PARAMS,
        name="pack",
    )(*map(vmem, (elevation, equilibrium, depth, land_mask, friction, after)))


def tile_rows(ref, at, size, nxt):
    here = ref[at : at + size, :]
    after = ref[nxt : nxt + 8, :]
    return here, jnp.concatenate([here[1:], after[0:1]], axis=0)


def east(x):
    return rolled(x, -1, 1)


def row_metric(at, size, width, rows):
    first = lax.axis_index("ty") * rows
    index = lax.broadcasted_iota(jnp.int32, (size, LANES), 0) + (first + at)
    ax = metric(index.astype(F32), rows * lax.axis_size("ty"))
    return ax, jnp.concatenate([ax] * (width // LANES), axis=1)


def first_kernel(e, q, d, mask, r, after, e1, send, keep, coef, var):
    del after
    kdev, _, rows, width = e.shape
    size = 16
    ws = omegas(kdev)
    last_v = [jnp.zeros((1, width), F32)] * (2 * kdev)
    for at in range(0, rows, size):
        nxt = min(at + size, rows - 8)
        _, ax = row_metric(at, size, width, rows)
        md, mn = tile_rows(mask, at, size, nxt)
        dd, dn = tile_rows(d, at, size, nxt)
        rd, rn = tile_rows(r, at, size, nxt)
        coef_u = (THETA * ax * ax) * (md * east(md) * (dd + east(dd)))
        coef_v = (THETA * AY * AY) * (md * mn * (dd + dn))
        coef[0, at : at + size, :], coef[1, at : at + size, :] = coef_u, coef_v
        r2u = rd + east(rd)
        r2v = rd + rn
        squ, sqv = r2u * r2u, r2v * r2v
        sum_u = sum_v = None
        for c in range(kdev):
            w2 = 2.0 * ws[c]
            wt = THETA * ws[c]
            er, ern = tile_rows(e.at[c, 0], at, size, nxt)
            ei, ein = tile_rows(e.at[c, 1], at, size, nxt)
            qr, qrn = tile_rows(q.at[c, 0], at, size, nxt)
            qi, qin = tile_rows(q.at[c, 1], at, size, nxt)
            zr, zi = er - qr, ei - qi
            gu = coef_u * recip(squ + w2 * w2)
            gv = coef_v * recip(sqv + w2 * w2)
            ur, ui = flux(zr - east(zr), zi - east(zi), gu, gu * r2u, w2)
            vr, vi = flux(zr - (ern - qrn), zi - (ein - qin), gv, gv * r2v, w2)
            uwr, uwi = rolled(ur, 1, 1), rolled(ui, 1, 1)
            vsr = jnp.concatenate([last_v[2 * c], vr[:-1]], axis=0)
            vsi = jnp.concatenate([last_v[2 * c + 1], vi[:-1]], axis=0)
            last_v[2 * c], last_v[2 * c + 1] = vr[-1:], vi[-1:]
            e1[c, 0, at : at + size, :] = md * (er + wt * ei - (ur - uwr) - (vr - vsr))
            e1[c, 1, at : at + size, :] = md * (ei - wt * er - (ui - uwi) - (vi - vsi))
            su = (ur + uwr) * (ur + uwr) + (ui + uwi) * (ui + uwi)
            sv = (vr + vsr) * (vr + vsr) + (vi + vsi) * (vi + vsi)
            sum_u = su if sum_u is None else sum_u + su
            sum_v = sv if sum_v is None else sum_v + sv
        inv = recip(dd)
        ia = recip(THETA * ax)
        total = (0.125 * ia * ia) * sum_u + (0.125 / (THETA * AY) ** 2) * sum_v
        var[at : at + size, :] = total * (inv * inv)
    half = rows // 2
    core = lax.rem(lax.axis_index("cons"), 2)
    send[:half, :] = var[pl.ds(pl.multiple_of((1 - core) * half, 8), half), :]
    keep[:half, :] = var[pl.ds(pl.multiple_of(core * half, 8), half), :]
    send[half:, :] = keep[half - 8 : half, :]
    keep[half:, :] = send[half - 8 : half, :]


def first_sweep(e, q, d, m, r, after):
    kdev, _, rows, width = e.shape
    half = pltpu.VMEM((rows // 2 + 8, width), F32)
    return pl.pallas_call(
        first_kernel,
        out_shape=(pltpu.VMEM(e.shape, F32), half, half, pltpu.VMEM((2, *d.shape), F32)),
        in_specs=[pl.BlockSpec(memory_space=pltpu.VMEM)] * 6,
        out_specs=[pl.BlockSpec(memory_space=pltpu.VMEM)] * 4,
        scratch_shapes=[pltpu.VMEM(d.shape, F32)],
        compiler_params=PARAMS,
        cost_estimate=pl.CostEstimate(flops=80 * e.size, bytes_accessed=160 * e.size, transcendentals=0),
        name="first_sweep",
    )(*map(vmem, (e, q, d, m, r, after)))


def add_kernel(a, b, *refs):
    refs[-1][...] = a[...] + b[...]


def added(a, b, *after):
    return pl.pallas_call(
        add_kernel,
        out_shape=pltpu.VMEM(a.shape, F32),
        in_specs=[pl.BlockSpec(memory_space=pltpu.VMEM)] * (2 + len(after)),
        out_specs=pl.BlockSpec(memory_space=pltpu.VMEM),
        compiler_params=PARAMS,
        name="added",
    )(vmem(a), vmem(b), *map(vmem, after))


def cut_kernel(a, b, after, *outs):
    del after
    at = 0
    for out in outs:
        here = slice(at, at + out.shape[0])
        out[...] = a[here, :] + b[here, :]
        at += out.shape[0]


def cut_sum(a, b, after):
    rows, width = a.shape
    large = pltpu.VMEM(((rows - 16) // 2, width), F32)
    return pl.pallas_call(
        cut_kernel,
        out_shape=(large, large, pltpu.VMEM((16, width), F32)),
        in_specs=[pl.BlockSpec(memory_space=pltpu.VMEM)] * 3,
        out_specs=[pl.BlockSpec(memory_space=pltpu.VMEM)] * 3,
        compiler_params=PARAMS,
        name="cut_sum",
    )(vmem(a), vmem(b), vmem(after))


def tree_sum(terms):
    while len(terms) > 1:
        terms = [a + b for a, b in zip(terms[::2], terms[1::2])]
    return terms[0]


def early_kernel(after, *refs):
    del after
    pieces, partner, outs = refs[:2], refs[2:4], refs[4:]
    thin = outs[0].shape[0]
    for k, out in enumerate(outs):
        part, at = divmod(k * thin, pieces[0].shape[0])
        out[...] = pieces[part][at : at + thin, :] + partner[part][at : at + thin, :]


def early_sums(pieces, partner, after):
    rows, width = pieces[0].shape
    count = 2 * rows // 16
    return pl.pallas_call(
        early_kernel,
        out_shape=(pltpu.VMEM((16, width), F32),) * count,
        in_specs=[pl.BlockSpec(memory_space=pltpu.VMEM)] * 5,
        out_specs=[pl.BlockSpec(memory_space=pltpu.VMEM)] * count,
        compiler_params=PARAMS,
        name="early_sums",
    )(*map(vmem, (after, *pieces, *partner)))


def join_kernel(tail, partner, both, after, *refs):
    del after
    *others, late, rims = refs
    late[...] = tail[:16, :] + partner[:16, :]
    terms = [x[...] for x in others]
    rims[...] = tree_sum([both[...], partner[16:, :] + terms[0], *[a + b for a, b in zip(terms[1::2], terms[2::2])]])


def joined(*args):
    width = args[0].shape[1]
    return pl.pallas_call(
        join_kernel,
        out_shape=(pltpu.VMEM((16, width), F32), pltpu.VMEM((8, width), F32)),
        in_specs=[pl.BlockSpec(memory_space=pltpu.VMEM)] * len(args),
        out_specs=[pl.BlockSpec(memory_space=pltpu.VMEM)] * 2,
        compiler_params=PARAMS,
        name="joined",
    )(*map(vmem, args))


def roles(a, b):
    even = lax.rem(lax.axis_index("tx"), 2) == 0
    return jnp.where(even, b, a), jnp.where(even, a, b)


def padded(x, pad):
    return jnp.concatenate([x, jnp.zeros((x.shape[0], pad - x.shape[1]), F32)], axis=1)


def merge_kernel(rows, f2, f1, mn, ms, send, mn_out, ms_out, my_out, send_out):
    width = mn.shape[1] - LANES
    fw, fe = roles(f1[...], padded(f2[...], f1.shape[1]))
    lane = lax.broadcasted_iota(jnp.int32, (MSG, LANES), 1)
    last = LANES - 1

    def ends(at):
        east_, west = fe[:, at // LANES * LANES :][:, :LANES], fw[:, at // LANES * LANES :][:, :LANES]
        east_, west = rolled(east_, -(at % LANES), 1), rolled(west, last - at % LANES, 1)
        return jnp.where(lane == 0, east_, jnp.where(lane == last, west, 0.0))

    mn_out[:, :width] = mn[:, :width]
    ms_out[:, :width] = ms[:, :width]
    mn_out[:, width:] = ends(rows - 1)
    ms_out[:, width:] = ends(0)
    low = lax.axis_index("ty") == 0
    my_out[...] = jnp.where(low, mn_out[...], ms_out[...])
    send_out[...] = send[...]


def merge(rows, f1, f2, mn, ms, send):
    out = pltpu.VMEM(mn.shape, F32)
    return pl.pallas_call(
        functools.partial(merge_kernel, rows),
        out_shape=(out, out, out, pltpu.VMEM(send.shape, F32)),
        in_specs=[pl.BlockSpec(memory_space=pltpu.VMEM)] * 5,
        out_specs=[pl.BlockSpec(memory_space=pltpu.VMEM)] * 4,
        compiler_params=PARAMS,
        name="merge",
    )(*map(vmem, (f2, f1, mn, ms, send)))


def strip_omega(shape, ws):
    odd = lax.rem(lax.broadcasted_iota(jnp.int32, shape, 0), 2)
    return jnp.where(odd == 0, ws[0], ws[1])


def strip_sweep(low, high, ws, g_across, g_along):
    none = jnp.zeros((2, low.shape[1]), F32)

    def field(at):
        return jnp.concatenate([none, low[at : at + 2], high[at : at + 2], none], axis=0)

    def single(at):
        a, b = low[at : at + 1], high[at : at + 1]
        return jnp.concatenate([none, a, a, b, b, none], axis=0)

    def given(at):
        return jnp.concatenate([low[at : at + 2], none, high[at : at + 2], none], axis=0)

    zr, zi, er, ei = field(0), field(2), field(8), field(10)
    r, d, m = single(12), single(13), single(14)
    w = strip_omega(zr.shape, ws)
    w2 = 2.0 * w
    wt = THETA * w
    up = lambda x: rolled(x, -2, 0)
    nx = lambda x: rolled(x, -1, 1)
    coef_a = (THETA * g_across * g_across) * (m * up(m) * (d + up(d)))
    coef_l = (THETA * g_along * g_along) * (m * nx(m) * (d + nx(d)))
    ar, ai = face(zr, zi, up(zr), up(zi), r + up(r), coef_a, w2)
    middle = lax.broadcasted_iota(jnp.int32, zr.shape, 0) // 2 == 1
    ar, ai = jnp.where(middle, ar, given(4)), jnp.where(middle, ai, given(6))
    lr, li = face(zr, zi, nx(zr), nx(zi), r + nx(r), coef_l, w2)
    abr, abi = rolled(ar, 2, 0), rolled(ai, 2, 0)
    lbr, lbi = rolled(lr, 1, 1), rolled(li, 1, 1)
    e1r = m * (er + wt * ei - (ar - abr) - (lr - lbr))
    e1i = m * (ei - wt * er - (ai - abi) - (li - lbi))
    sa = (ar + abr) * (ar + abr) + (ai + abi) * (ai + abi)
    sl = (lr + lbr) * (lr + lbr) + (li + lbi) * (li + lbi)
    inv = recip(jnp.maximum(d, TINY_DEPTH))
    ia = recip(THETA * g_across)
    il = recip(THETA * g_along)
    var = 0.125 * (ia * ia * sa + il * il * sl) * (inv * inv)
    var = var + rolled(var, -1, 0)
    z1r = e1r - (er - zr)
    z1i = e1i - (ei - zi)
    return (z1r, z1i, d, coef_a, e1r, e1i), var


def strips(rows, m2, m1, f2, f1, mn, ms, fn_ref, fs_ref):
    kdev = 2
    width = mn.shape[1] - LANES
    pad = m1.shape[1]
    ws = omegas(kdev)
    ty, count = lax.axis_index("ty"), lax.axis_size("ty")
    first = (ty * rows).astype(F32)
    total = rows * count
    fn = jnp.where(ty < count - 1, fn_ref[...], 0.0)
    fs = jnp.where(ty > 0, fs_ref[...], 0.0)

    ay = AY
    line = lax.broadcasted_iota(jnp.int32, (8, LANES), 0) // 2
    out = []
    for low, high, start in ((fs, ms[...], -2), (mn[...], fn, rows - 2)):
        ax = metric((line + start).astype(F32) + first, total)
        ax = jnp.concatenate([ax] * (low.shape[1] // LANES), axis=1)
        out.append(strip_sweep(low, high, ws, ay, ax))

    mw, me = roles(m1[...], padded(m2[...], pad))
    fw, fe = roles(f1[...], padded(f2[...], pad))
    hi = rows - (pad - LANES)
    last = LANES - 1
    lane = lax.broadcasted_iota(jnp.int32, (MSG, LANES), 1)

    def ended(msg, block, at):
        end = msg[:, pad - LANES :]
        end = jnp.where(lane == hi, rolled(fn[:, block : block + LANES], hi - at, 1), end)
        end = jnp.where(lane == last, rolled(fs[:, block : block + LANES], last - at, 1), end)
        return jnp.concatenate([msg[:, : pad - LANES], end], axis=1)

    low_w, high_w = ended(fw, width, last), ended(mw, 0, 0)
    low_e, high_e = ended(me, width - LANES, last), ended(fe, width, 0)
    row = lax.broadcasted_iota(jnp.int32, (8, pad), 1).astype(F32) + first
    ax = metric(jnp.minimum(row, first + rows), total)
    for low, high in ((low_w, high_w), (low_e, high_e)):
        out.append(strip_sweep(low, high, ws, ax, ay))
    return out


def rim_kernel(rows, after, *refs):
    del after
    *refs, row_sums, col_sums = refs
    width, pad = row_sums.shape[1], refs[1].shape[1]
    for k, (_, var) in enumerate(strips(rows, *refs)):
        for p in range(2):
            if k < 2:
                row_sums[2 * k + p, :] = var[2 + 2 * p, :width]
            else:
                col_sums[k - 2, p * pad : (p + 1) * pad] = var[2 + 2 * p, :]
    col_sums[2:, :] = jnp.zeros((2, width), F32)


def strips_kernel(rows, *refs):
    for out, (held, _) in zip(refs[-4:], strips(rows, *refs[:-4])):
        for k, x in enumerate(held):
            out[8 * k : 8 * k + 8, :] = x


def rim(rows, late, *messages):
    width = late.shape[1]
    return pl.pallas_call(
        functools.partial(rim_kernel, rows),
        out_shape=(pltpu.VMEM((4, width), F32),) * 2,
        in_specs=[pl.BlockSpec(memory_space=pltpu.VMEM)] * 9,
        out_specs=[pl.BlockSpec(memory_space=pltpu.VMEM)] * 2,
        compiler_params=PARAMS,
        name="rim",
    )(*map(vmem, (late, *messages)))


def stack_kernel(a, b, out):
    out[: a.shape[0], :] = a[...]
    out[a.shape[0] :, :] = b[...]


def stacked(a, b):
    return pl.pallas_call(
        stack_kernel,
        out_shape=pltpu.VMEM((a.shape[0] + b.shape[0], a.shape[1]), F32),
        in_specs=[pl.BlockSpec(memory_space=pltpu.VMEM)] * 2,
        out_specs=pl.BlockSpec(memory_space=pltpu.VMEM),
        compiler_params=PARAMS,
        name="stacked",
    )(vmem(a), vmem(b))


def held_strips(rows, *messages):
    row = pltpu.VMEM((48, messages[4].shape[1]), F32)
    col = pltpu.VMEM((48, messages[1].shape[1]), F32)
    return pl.pallas_call(
        functools.partial(strips_kernel, rows),
        out_shape=(row, row, col, col),
        in_specs=[pl.BlockSpec(memory_space=pltpu.VMEM)] * 8,
        out_specs=[pl.BlockSpec(memory_space=pltpu.VMEM)] * 4,
        compiler_params=PARAMS,
        name="held_strips",
    )(*map(vmem, messages))


def prepare_kernel(e1_in, q, m, ss, sn, sw, se, du, dv, base, e1, cols):
    kdev, _, rows, width = e1_in.shape
    size = 16
    ws = omegas(kdev)
    e1[...] = e1_in[...]
    for p in range(2):
        cols[2 * p : 2 * p + 2, :] = sw[8 * (4 + p) + 4 : 8 * (4 + p) + 6, :]
        cols[4 + 2 * p : 6 + 2 * p, :] = se[8 * (4 + p) + 2 : 8 * (4 + p) + 4, :]
    turned = cols[...].T
    lane = lax.broadcasted_iota(jnp.int32, (rows, LANES), 1)
    left, right = slice(0, LANES), slice(width - LANES, width)
    last = LANES - 1
    for p in range(2):
        for c in range(kdev):
            e1[c, p, 0:1, :] = ss[8 * (4 + p) + 4 + c : 8 * (4 + p) + 5 + c, :width]
            e1[c, p, rows - 1 : rows, :] = sn[8 * (4 + p) + 2 + c : 8 * (4 + p) + 3 + c, :width]
            k = 2 * p + c
            e1[c, p, :, left] = jnp.where(lane == 0, rolled(turned[:rows], -k, 1), e1[c, p, :, left])
            k = 4 + 2 * p + c
            e1[c, p, :, right] = jnp.where(lane == last, rolled(turned[:rows], last - k, 1), e1[c, p, :, right])
    for at in range(0, rows, size):
        nxt = min(at + size, rows - 8)
        here = slice(at, at + size)
        md = m[here, :]
        for c in range(kdev):
            wt = THETA * ws[c]
            er, ern = tile_rows(e1.at[c, 0], at, size, nxt)
            ei, ein = tile_rows(e1.at[c, 1], at, size, nxt)
            qr, qrn = tile_rows(q.at[c, 0], at, size, nxt)
            qi, qin = tile_rows(q.at[c, 1], at, size, nxt)
            zr, zi = er - qr, ei - qi
            du[c, 0, here, :] = zr - east(zr)
            du[c, 1, here, :] = zi - east(zi)
            dv[c, 0, here, :] = zr - (ern - qrn)
            dv[c, 1, here, :] = zi - (ein - qin)
            base[c, 0, here, :] = md * (er + wt * ei)
            base[c, 1, here, :] = md * (ei - wt * er)


def prepare(e1, q, m, ss, sn, sw, se):
    plane = pltpu.VMEM(e1.shape, F32)
    return pl.pallas_call(
        prepare_kernel,
        out_shape=(plane, plane, plane),
        in_specs=[pl.BlockSpec(memory_space=pltpu.VMEM)] * 7,
        out_specs=[pl.BlockSpec(memory_space=pltpu.VMEM)] * 3,
        scratch_shapes=[pltpu.VMEM(e1.shape, F32), pltpu.VMEM((LANES, sw.shape[1]), F32)],
        compiler_params=PARAMS,
        cost_estimate=pl.CostEstimate(flops=40 * e1.size, bytes_accessed=160 * e1.size, transcendentals=0),
        name="prepare",
    )(*map(vmem, (e1, q, m, ss, sn, sw, se)))


def rate(var, d):
    s = var + BACKGROUND
    return (DRAG * (s * lax.rsqrt(s))) * recip(d)


def sweep_tile(row, size, r, r_north, du, dv, base, coef, m, turned, ws, last_v, top):
    kdev, width = du.shape[0], du.shape[3]
    here = pl.ds(row, size)
    edges = turned[here, :]
    md = m[here, :]
    coef_u, coef_v = coef[0, here, :], coef[1, here, :]
    r2u = r + east(r)
    r2v = r + r_north
    squ, sqv = r2u * r2u, r2v * r2v
    lane = lax.broadcasted_iota(jnp.int32, (size, LANES), 1)
    last = LANES - 1

    def with_east(u, k):
        block = jnp.where(lane == last, rolled(edges, last - k, 1), u[:, width - LANES :])
        return jnp.concatenate([u[:, : width - LANES], block], axis=1)

    def from_west(u, k):
        u = rolled(u, 1, 1)
        block = jnp.where(lane == 0, rolled(edges, -k, 1), u[:, :LANES])
        return jnp.concatenate([block, u[:, LANES:]], axis=1)

    planes, out_v = {}, {}
    for c in range(kdev):
        w2 = 2.0 * ws[c]
        gu = coef_u * recip(squ + w2 * w2)
        gv = coef_v * recip(sqv + w2 * w2)
        u = flux(du[c, 0, here, :], du[c, 1, here, :], gu, gu * r2u, w2)
        v = flux(dv[c, 0, here, :], dv[c, 1, here, :], gv, gv * r2v, w2)
        for p in range(2):
            up, vp = with_east(u[p], 4 + 2 * p + c), v[p]
            if top is not None:
                vp = jnp.concatenate([vp[:-1], top(c, p, vp[-1:])], axis=0)
            uw = from_west(up, 2 * p + c)
            vs = jnp.concatenate([last_v[c, p], vp[:-1]], axis=0)
            out_v[c, p] = vp[-1:]
            planes[c, p] = base[c, p, here, :], md * ((up - uw) + (vp - vs))
    return planes, out_v


def pairs(kdev):
    return [(c, p) for c in range(kdev) for p in range(2)]


def half_rate(var, rims, turned, d, row, low, half):
    here = pl.ds(row, half)
    edges = turned[here, :]
    width = var.shape[1]
    index = lax.broadcasted_iota(jnp.int32, (8, width), 0)
    first = jnp.where(low & (index == 0), rims[1:2], var[:8])
    final = jnp.where(jnp.logical_not(low) & (index == 7), rims[2:3], var[half - 8 :])
    var = jnp.concatenate([first, var[8 : half - 8], final], axis=0)
    lane = lax.broadcasted_iota(jnp.int32, (half, LANES), 1)
    left = jnp.where(lane == 0, rolled(edges, -8, 1), var[:, :LANES])
    right = jnp.where(lane == LANES - 1, rolled(edges, LANES - 1 - 9, 1), var[:, width - LANES :])
    return rate(jnp.concatenate([left, var[:, LANES : width - LANES], right], axis=1), d[here, :])


def own_kernel(du, dv, base, coef, d, m, late, rims_ref, ss, sn, sw, se, *refs):
    *mine, first_part, update, fric, vs_out, vn_out, turned, cols = refs
    kdev, _, half, width = update.shape
    pad = sw.shape[1]
    ws = omegas(kdev)
    core = lax.rem(lax.axis_index("cons"), 2)
    low = core == 0
    rims = rims_ref[...]

    def edge(strip, var_a, var_b):
        zr, zi, dep, ca = (strip[8 * k : 8 * k + 8, :] for k in range(4))
        var = jnp.concatenate([var_a, var_a, var_a, var_a, var_b, var_b, var_b, var_b], axis=0)
        f = rate(var, jnp.maximum(dep, TINY_DEPTH))
        up = lambda x: rolled(x, -2, 0)
        w2 = 2.0 * strip_omega(zr.shape, ws)
        return face(zr, zi, up(zr), up(zi), f + up(f), ca, w2)

    none = jnp.zeros((1, LANES), F32)
    wide = lambda x: jnp.concatenate([x, none], axis=1)
    south = edge(ss, wide(rims[0:1]), wide(rims[1:2]))
    north = edge(sn, wide(rims[2:3]), wide(rims[3:4]))
    west = edge(sw, rims[4:5, :pad], rims[4:5, pad : 2 * pad])
    east_ = edge(se, rims[5:6, :pad], rims[5:6, pad : 2 * pad])
    for p in range(2):
        cols[2 * p : 2 * p + 2, :] = west[p][2:4]
        cols[4 + 2 * p : 6 + 2 * p, :] = east_[p][2:4]
        for c in range(kdev):
            vs_out[2 * c + p : 2 * c + p + 1, :] = south[p][2 + c : 3 + c, :width]
            vn_out[2 * c + p : 2 * c + p + 1, :] = north[p][2 + c : 3 + c, :width]
    cols[8:9, :] = rims[4:5, pad : 2 * pad]
    cols[9:10, :] = rims[5:6, :pad]
    turned[...] = cols[...].T

    first = pl.multiple_of(core * half, 8)
    var = jnp.concatenate([x[...] for x in mine] + [late[:8, :]], axis=0)
    fric[...] = half_rate(var, rims, turned, d, first, low, half)
    size = 24
    last_v = {(c, p): jnp.where(low, vs_out[2 * c + p : 2 * c + p + 1, :], 0.0) for c, p in pairs(kdev)}

    def top(c, p, own):
        return jnp.where(low, 0.0, vn_out[2 * c + p : 2 * c + p + 1, :])

    for at in range(0, half, size):
        r, rn = tile_rows(fric, at, size, min(at + size, half - 8))
        planes, last_v = sweep_tile(
            pl.multiple_of(first + at, 8), size, r, rn, du, dv, base, coef, m, turned, ws, last_v,
            top if at + size == half else None,
        )
        for c, p in pairs(kdev):
            first_part[c, p, at : at + size, :], update[c, p, at : at + size, :] = planes[c, p]


def own_half(*args):
    kdev, _, rows, width = args[0].shape
    pad = args[10].shape[1]
    line = pltpu.VMEM((8, width), F32)
    return pl.pallas_call(
        own_kernel,
        out_shape=(
            pltpu.VMEM((kdev, 2, rows // 2, width), F32),
            pltpu.VMEM((kdev, 2, rows // 2, width), F32),
            pltpu.VMEM((rows // 2, width), F32),
            line,
            line,
            pltpu.VMEM((pad, LANES), F32),
        ),
        in_specs=[pl.BlockSpec(memory_space=pltpu.VMEM)] * len(args),
        out_specs=[pl.BlockSpec(memory_space=pltpu.VMEM)] * 6,
        scratch_shapes=[pltpu.VMEM((LANES, pad), F32)],
        compiler_params=PARAMS,
        name="own_half",
    )(*map(vmem, args))


def other_kernel(du, dv, base, coef, d, m, late, rims, eta_own, fric_own, vs, vn, turned, *refs):
    *other, eta_out, fric_out, eta, fric, fixed, sems = refs
    kdev, _, half, width = eta.shape
    ws = omegas(kdev)
    core = lax.rem(lax.axis_index("cons"), 2)
    own_low = core == 0
    own, first = pl.multiple_of(core * half, 8), pl.multiple_of((1 - core) * half, 8)
    copies = []

    def put(src, dst):
        copy = pltpu.make_async_copy(src, dst, sems.at[len(copies)])
        copy.start()
        copies.append(copy)

    skip = pl.multiple_of(core * 8, 8)
    put(
        eta_own.at[:, :, pl.ds(skip, half - 8), :],
        eta_out.at[:, :, pl.ds(pl.multiple_of(own + skip, 8), half - 8), :],
    )
    put(fric_own, fric_out.at[pl.ds(own, half), :])
    fric[pl.ds(own, half), :] = fric_own[...]
    fric[pl.ds(first, half), :] = half_rate(
        jnp.concatenate([x[...] for x in other] + [late[8:, :]], axis=0),
        rims[...], turned, d, first, jnp.logical_not(own_low), half,
    )
    put(fric.at[pl.ds(first, half), :], fric_out.at[pl.ds(first, half), :])

    r, rn = tile_rows(fric, half - 8, 8, half)
    r2 = r + rn
    between = {}
    for c in range(kdev):
        w2 = 2.0 * ws[c]
        g = coef[1, half - 8 : half, :] * recip(r2 * r2 + w2 * w2)
        v = flux(dv[c, 0, half - 8 : half, :], dv[c, 1, half - 8 : half, :], g, g * r2, w2)
        for p in range(2):
            between[c, p] = v[p][7:8]
    index = lax.broadcasted_iota(jnp.int32, (8, width), 0)
    at_face = index == jnp.where(own_low, 7, 0)
    sign = jnp.where(own_low, -1.0, 1.0)
    local = pl.ds(pl.multiple_of((1 - core) * (half - 8), 8), 8)
    border = pl.ds(pl.multiple_of(half - 8 + 8 * core, 8), 8)
    md = m[border, :]
    for c, p in pairs(kdev):
        fixed[c, p] = eta_own[c, p, local, :] + jnp.where(at_face, sign * (md * between[c, p]), 0.0)
    put(fixed, eta_out.at[:, :, border, :])

    size = 24
    rows = 2 * half
    last_v = {(c, p): jnp.where(own_low, between[c, p], vs[2 * c + p : 2 * c + p + 1, :]) for c, p in pairs(kdev)}

    def top(c, p, own_v):
        return jnp.where(own_low, vn[2 * c + p : 2 * c + p + 1, :], own_v)

    for at in range(0, half, size):
        row = pl.multiple_of(first + at, 8)
        r = fric[pl.ds(row, size), :]
        after = fric[pl.ds(pl.multiple_of(jnp.minimum(row + size, rows - 8), 8), 8), :]
        rn = jnp.concatenate([r[1:], after[0:1]], axis=0)
        planes, last_v = sweep_tile(
            row, size, r, rn, du, dv, base, coef, m, turned, ws, last_v, top if at + size == half else None
        )
        for c, p in pairs(kdev):
            eta[c, p, at : at + size, :] = planes[c, p][0] - planes[c, p][1]
        put(eta.at[:, :, at : at + size, :], eta_out.at[:, :, pl.ds(row, size), :])
    for copy in copies:
        copy.wait()


def other_half(*args):
    du, d = args[0], args[4]
    kdev, _, rows, width = du.shape
    return pl.pallas_call(
        other_kernel,
        out_shape=(jax.ShapeDtypeStruct(du.shape, F32), jax.ShapeDtypeStruct(d.shape, F32)),
        in_specs=[pl.BlockSpec(memory_space=pltpu.VMEM)] * len(args),
        out_specs=[pl.BlockSpec(memory_space=pltpu.HBM)] * 2,
        scratch_shapes=[
            pltpu.VMEM((kdev, 2, rows // 2, width), F32),
            pltpu.VMEM(d.shape, F32),
            pltpu.VMEM((kdev, 2, 8, width), F32),
            pltpu.SemaphoreType.DMA((4 + rows // 2 // 24,)),
        ],
        compiler_params=PARAMS,
        name="other_half",
    )(*map(vmem, args))


def swapped(x, axis, bit):
    return lax.ppermute(x, axis, [(i, i ^ bit) for i in range(lax.axis_size(axis))])


def body(elevation, equilibrium, depth, land_mask, friction_prev):
    rows = depth.shape[0]
    ntx, nty, ncons = (lax.axis_size(a) for a in ("tx", "ty", "cons"))
    fields = (elevation, equilibrium, depth, land_mask, friction_prev)
    m2, m1 = pack_columns(*fields)
    elev, equil, depth, mask, fric = elevation, equilibrium, depth, land_mask, friction_prev
    mask, mn, ms = pack(*fields, m1)
    f2 = lax.ppermute(m2, "tx", [(i, (i - 1 if i % 2 == 0 else i + 1) % ntx) for i in range(ntx)])
    f1 = swapped(m1, "tx", 1)
    e1, send, keep, coef = first_sweep(elev, equil, depth, mask, fric, m1)
    mn, ms, my, send = merge(rows, f1, f2, mn, ms, send)
    recv = swapped(send, "cons", 1)
    if nty == 2:
        fn = fs = swapped(my, "ty", 1)
    else:
        fn = lax.ppermute(ms, "ty", [(i, i - 1) for i in range(1, nty)])
        fs = lax.ppermute(mn, "ty", [(i, i + 1) for i in range(nty - 1)])
    first, second, late = cut_sum(recv, keep, my)
    messages = (m2, m1, f2, f1, mn, ms, fn, fs)
    rims = jnp.concatenate(rim(rows, late, *messages), axis=0)
    tail = stacked(late, rims)
    ss, sn, sw, se = held_strips(rows, *messages)
    prepared = prepare(e1, equil, mask, ss, sn, sw, se)
    partner = [swapped(x, "cons", 2) for x in (first, second, tail)]
    others = [swapped(rims, "cons", k) for k in range(1, ncons) if k != 2]
    both = added(rims, others[0], prepared[2])
    mine = early_sums((first, second), partner[:2], both)
    bit = 4
    while bit < ncons:
        mine = [added(x, swapped(x, "cons", bit)) for x in mine]
        tail, partner[2] = added(tail, partner[2]), swapped(added(tail, partner[2]), "cons", bit)
        bit *= 2
    other = [swapped(x, "cons", 1) for x in mine]
    late, rims = joined(tail, partner[2], both, other[0], *others[1:])
    fields = (*prepared, coef, depth, mask, late, rims)
    first_part, update, *own = own_half(*fields, ss, sn, sw, se, *mine)
    return other_half(*fields, first_part - update, *own, *other)


def solution(mesh):
    return jax.shard_map(
        body,
        mesh=mesh,
        in_specs=(
            P("cons", None, "ty", "tx"),
            P("cons", None, "ty", "tx"),
            P("ty", "tx"),
            P("ty", "tx"),
            P("ty", "tx"),
        ),
        out_specs=(P("cons", None, "ty", "tx"), P("ty", "tx")),
        check_vma=False,
    )
```

profile of v0, /device:TPU:0, one launch (start us, length us, event | category | flops | bytes accessed | tf_op | source)
XLA Modules:
  0.0 23.4 jit_solution(17567981811781665267)
XLA Ops:
  0.6 0.0 copy-start.2
  0.6 0.0 copy-start
  0.7 0.0 copy-start.3
  0.7 0.0 copy-start.1
  0.7 0.0 copy-start.4
  0.7 2.0 %pack_columns.1 = (f32[16,144]{1,0:T(8,128)S(1)}, f32[16,256]{1,0:T(8,128)S(1)}) custom-call(f32[2,2,144,512]{3,2,1,0:T(8,128)} %e.3, f32[2,2,144,512]{3,2,1,0:T(8,128)} %q.5, f32[144,512]{1,0:T(8,128)} %d.7, s32[144,512]{1,0:T(8,128)} %ints.1, f32[144,512]{1,0:T(8,128)} %r.3), custom_call_target="tpu_custom_call" | custom-call | tf_op jit(solution)/shard_map/pack_columns/pallas_call | solution.py:126
  2.7 3.1 %collective-permute-start.1 = (f32[16,256]{1,0:T(8,128)S(1)}, f32[16,256]{1,0:T(8,128)S(1)}, u32[]{:S(2)}, u32[]{:S(2)}) collective-permute-start(f32[16,256]{1,0:T(8,128)S(1)} %get-tuple-element.39.after.refs_1_), channel_id=1, source_target_pairs={{0,1},{1,0},{2,3},{3,2},{4,5},{5,4},{6,7},{7,6},{8,9},{9,8},{10,11... | collective-permute-start | bytes 49160 | tf_op jit(solution)/shard_map/ppermute | solution.py:819
  5.8 2.5 %collective-permute-start = (f32[16,144]{1,0:T(8,128)S(1)}, f32[16,144]{1,0:T(8,128)S(1)}, u32[]{:S(2)}, u32[]{:S(2)}) collective-permute-start(f32[16,144]{1,0:T(8,128)S(1)} %get-tuple-element.42.refs_0_), channel_id=1, source_target_pairs={{0,3},{1,2},{2,1},{3,0},{4,7},{5,6},{6,5},{7,4},{8,11},{9,10},{10,... | collective-permute-start | bytes 27656 | tf_op jit(solution)/shard_map/ppermute | solution.py:829
  8.3 0.0 copy-done.2
  8.3 0.0 copy-done
  8.3 0.0 copy-done.3
  8.3 0.0 copy-done.1
  8.3 0.0 copy-done.4
  8.3 0.1 pack.1
  8.4 2.1 %first_sweep.1 = (f32[2,2,144,512]{3,2,1,0:T(8,128)S(1)}, f32[80,512]{1,0:T(8,128)S(1)}, f32[80,512]{1,0:T(8,128)S(1)}, f32[2,144,512]{2,1,0:T(8,128)S(1)}) custom-call(f32[2,2,144,512]{3,2,1,0:T(8,128)S(1)} %copy-done.1, f32[2,2,144,512]{3,2,1,0:T(8,128)S(1)} %copy-done, f32[144,512]{1,0:T(8,128)S(1)} %copy-done.2, ...), custom_call_target="tpu_custom_call" | custom-call | flops 23592960 | bytes 47185920 | tf_op jit(solution)/shard_map/first_sweep/pallas_call | solution.py:257
  10.5 0.8 %collective-permute-done.f2.refs_2_ = f32[16,144]{1,0:T(8,128)S(1)} collective-permute-done((f32[16,144]{1,0:T(8,128)S(1)}, f32[16,144]{1,0:T(8,128)S(1)}, u32[]{:S(2)}, u32[]{:S(2)}) %collective-permute-start) | collective-permute-done | bytes 9248 | tf_op jit(solution)/shard_map/ppermute | solution.py:829
  11.3 0.0 collective-permute-done.1.f1.refs_3_
  11.3 0.1 merge.1
  11.4 0.0 collective-permute-start.3
  11.4 1.6 %collective-permute-start.2 = (f32[16,640]{1,0:T(8,128)S(1)}, f32[16,640]{1,0:T(8,128)S(1)}, u32[]{:S(2)}, u32[]{:S(2)}) collective-permute-start(f32[16,640]{1,0:T(8,128)S(1)} %get-tuple-element.48.after), channel_id=1, source_target_pairs={{0,4},{4,0},{1,5},{5,1},{2,6},{6,2},{3,7},{7,3},{8,12},{12,8},{9,1... | collective-permute-start | bytes 122888 | tf_op jit(solution)/shard_map/ppermute | solution.py:819
  13.0 0.0 collective-permute-done.3.a
  13.0 1.6 %collective-permute-start.6 = (f32[32,512]{1,0:T(8,128)S(1)}, f32[32,512]{1,0:T(8,128)S(1)}, u32[]{:S(2)}, u32[]{:S(2)}) collective-permute-start(f32[32,512]{1,0:T(8,128)S(1)} %get-tuple-element.62.refs_0_), channel_id=1, source_target_pairs={{0,16},{8,24},{16,0},{24,8},{1,17},{9,25},{17,1},{25,9},{2,18},{10... | collective-permute-start | bytes 196616 | tf_op jit(solution)/shard_map/ppermute | solution.py:819
  14.6 0.5 %collective-permute-start.7 = (f32[32,512]{1,0:T(8,128)S(1)}, f32[32,512]{1,0:T(8,128)S(1)}, u32[]{:S(2)}, u32[]{:S(2)}) collective-permute-start(f32[32,512]{1,0:T(8,128)S(1)} %get-tuple-element.63.refs_1_), channel_id=1, source_target_pairs={{0,16},{8,24},{16,0},{24,8},{1,17},{9,25},{17,1},{25,9},{2,18},{10... | collective-permute-start | bytes 196616 | tf_op jit(solution)/shard_map/ppermute | solution.py:819
  15.1 0.4 %collective-permute-done.2.refs_6_.refs_7_ = f32[16,640]{1,0:T(8,128)S(1)} collective-permute-done((f32[16,640]{1,0:T(8,128)S(1)}, f32[16,640]{1,0:T(8,128)S(1)}, u32[]{:S(2)}, u32[]{:S(2)}) %collective-permute-start.2) | collective-permute-done | bytes 40992 | tf_op jit(solution)/shard_map/ppermute | solution.py:819
  15.5 0.3 %rim.1 = (f32[4,512]{1,0:T(4,128)S(1)}, f32[4,512]{1,0:T(4,128)S(1)}) custom-call(f32[16,512]{1,0:T(8,128)S(1)} %get-tuple-element.59.after.a, f32[16,144]{1,0:T(8,128)S(1)} %get-tuple-element.42.refs_0_, f32[16,256]{1,0:T(8,128)S(1)} %get-tuple-element.39.after.refs_1_, f32[16,144]{1,0:T(8,128)S(1)} %collective-permute-done.f2.refs_2_, ...), custom_call_target="tpu_custom_call" | custom-call | tf_op jit(solution)/shard_map/rim/pallas_call | solution.py:503
  15.8 0.1 collective-permute-start.5
  15.9 1.6 %collective-permute-start.4 = (f32[24,512]{1,0:T(8,128)S(1)}, f32[24,512]{1,0:T(8,128)S(1)}, u32[]{:S(2)}, u32[]{:S(2)}) collective-permute-start(f32[24,512]{1,0:T(8,128)S(1)} %stacked.1.tail), channel_id=1, source_target_pairs={{0,16},{8,24},{16,0},{24,8},{1,17},{9,25},{17,1},{25,9},{2,18},{10... | collective-permute-start | bytes 147464 | tf_op jit(solution)/shard_map/ppermute | solution.py:819
  17.5 0.3 %collective-permute-start.9 = (f32[8,512]{1,0:T(8,128)S(1)}, f32[8,512]{1,0:T(8,128)S(1)}, u32[]{:S(2)}, u32[]{:S(2)}) collective-permute-start(f32[8,512]{1,0:T(8,128)S(1)} %pad_maximum_fusion.b.a), channel_id=1, source_target_pairs={{0,24},{8,16},{16,8},{24,0},{1,25},{9,17},{17,9},{25,1},{2,26},{10... | collective-permute-start | bytes 49160 | tf_op jit(solution)/shard_map/ppermute | solution.py:819
  17.8 0.3 %held_strips.1 = (f32[48,640]{1,0:T(8,128)S(1)}, f32[48,640]{1,0:T(8,128)S(1)}, f32[48,256]{1,0:T(8,128)S(1)}, f32[48,256]{1,0:T(8,128)S(1)}) custom-call(f32[16,144]{1,0:T(8,128)S(1)} %get-tuple-element.42.refs_0_, f32[16,256]{1,0:T(8,128)S(1)} %get-tuple-element.39.after.refs_1_, f32[16,144]{1,0:T(8,128)S(1)} %collective-permute-done.f2.refs_2_, ...), custom_call_target="tpu_custom_call" | custom-call | tf_op jit(solution)/shard_map/held_strips/pallas_call | solution.py:532
  18.0 0.8 %prepare.1 = (f32[2,2,144,512]{3,2,1,0:T(8,128)S(1)}, f32[2,2,144,512]{3,2,1,0:T(8,128)S(1)}, f32[2,2,144,512]{3,2,1,0:T(8,128)S(1)}) custom-call(f32[2,2,144,512]{3,2,1,0:T(8,128)S(1)} %get-tuple-element.41.e1_in, f32[2,2,144,512]{3,2,1,0:T(8,128)S(1)} %copy-done, f32[144,512]{1,0:T(8,128)S(1)} %get-tuple-element.40.mask.m, ...), custom_call_target="tpu_custom_call" | custom-call | flops 11796480 | bytes 47185920 | tf_op jit(solution)/shard_map/prepare/pallas_call | solution.py:583
  18.8 0.0 collective-permute-done.5.b
  18.8 0.0 collective-permute-done.6.refs_2_
  18.8 0.1 collective-permute-done.7.refs_3_
  18.9 0.4 %collective-permute-start.8 = (f32[16,512]{1,0:T(8,128)S(1)}, f32[16,512]{1,0:T(8,128)S(1)}, u32[]{:S(2)}, u32[]{:S(2)}) collective-permute-start(f32[16,512]{1,0:T(8,128)S(1)} %get-tuple-element.64.refs_0_), channel_id=1, source_target_pairs={{0,8},{8,0},{16,24},{24,16},{1,9},{9,1},{17,25},{25,17},{2,10},{10... | collective-permute-start | bytes 98312 | tf_op jit(solution)/shard_map/ppermute | solution.py:819
  19.3 0.2 collective-permute-start.10
  19.5 0.3 %collective-permute-start.11 = (f32[16,512]{1,0:T(8,128)S(1)}, f32[16,512]{1,0:T(8,128)S(1)}, u32[]{:S(2)}, u32[]{:S(2)}) collective-permute-start(f32[16,512]{1,0:T(8,128)S(1)} %get-tuple-element.68.refs_2_), channel_id=1, source_target_pairs={{0,8},{8,0},{16,24},{24,16},{1,9},{9,1},{17,25},{25,17},{2,10},{10... | collective-permute-start | bytes 98312 | tf_op jit(solution)/shard_map/ppermute | solution.py:819
  19.8 0.8 %collective-permute-done.9.refs_0_ = f32[8,512]{1,0:T(8,128)S(1)} collective-permute-done((f32[8,512]{1,0:T(8,128)S(1)}, f32[8,512]{1,0:T(8,128)S(1)}, u32[]{:S(2)}, u32[]{:S(2)}) %collective-permute-start.9) | collective-permute-done | bytes 16416 | tf_op jit(solution)/shard_map/ppermute | solution.py:819
  20.6 0.2 collective-permute-start.12
  20.8 0.0 collective-permute-done.4.partner
  20.8 0.0 collective-permute-done.8.after.refs_0_
  20.8 0.7 %own_half.1 = (f32[2,2,72,512]{3,2,1,0:T(8,128)S(1)}, f32[2,2,72,512]{3,2,1,0:T(8,128)S(1)}, f32[72,512]{1,0:T(8,128)S(1)}, f32[8,512]{1,0:T(8,128)S(1)}, f32[8,512]{1,0:T(8,128)S(1)}, /*index=5*/f32[256,128]{1,0:T(8,128)S(1)}) custom-call(f32[2,2,144,512]{3,2,1,0:T(8,128)S(1)} %get-tuple-element.53.du, f32[2,2,144,512]{3,2,1,0:T(8,128)S(1)} %get-tuple-element.54.dv, ...), custom_call_target="tpu_custom_call" | custom-call | tf_op jit(solution)/shard_map/own_half/pallas_call | solution.py:713
  21.6 0.1 sub.3.eta_own
  21.7 0.0 collective-permute-done.10.refs_1_
  21.7 0.0 collective-permute-done.11.refs_2_
  21.7 0.2 collective-permute-done.12.refs_3_
  21.9 1.5 %other_half.1 = (f32[2,2,144,512]{3,2,1,0:T(8,128)}, f32[144,512]{1,0:T(8,128)}) custom-call(f32[2,2,144,512]{3,2,1,0:T(8,128)S(1)} %get-tuple-element.53.du, f32[2,2,144,512]{3,2,1,0:T(8,128)S(1)} %get-tuple-element.54.dv, f32[2,2,144,512]{3,2,1,0:T(8,128)S(1)} %get-tuple-element.55.refs_0_.base, f32[2,144,512]{2,1,0:T(8,128)S(1)} %get-tuple-element.56.coef, ...), custom_call_target="tpu_custom_call" | custom-call | tf_op jit(solution)/shard_map/other_half/pallas_call | solution.py:802
  (6 shorter events, 0.1 us)
Async XLA Ops:
  0.6 7.6 %copy-start.2 = (f32[144,512]{1,0:T(8,128)S(1)}, f32[144,512]{1,0:T(8,128)}, u32[]{:S(2)}) copy-start(f32[144,512]{1,0:T(8,128)} %d.7) | copy-start | bytes 884740
  0.6 7.6 %copy-start = (f32[2,2,144,512]{3,2,1,0:T(8,128)S(1)}, f32[2,2,144,512]{3,2,1,0:T(8,128)}, u32[]{:S(2)}) copy-start(f32[2,2,144,512]{3,2,1,0:T(8,128)} %q.5) | copy-start | bytes 3538948
  0.7 7.6 %copy-start.3 = (f32[144,512]{1,0:T(8,128)S(1)}, f32[144,512]{1,0:T(8,128)}, u32[]{:S(2)}) copy-start(f32[144,512]{1,0:T(8,128)} %r.3) | copy-start | bytes 884740
  0.7 7.6 %copy-start.1 = (f32[2,2,144,512]{3,2,1,0:T(8,128)S(1)}, f32[2,2,144,512]{3,2,1,0:T(8,128)}, u32[]{:S(2)}) copy-start(f32[2,2,144,512]{3,2,1,0:T(8,128)} %e.3) | copy-start | bytes 3538948
  0.7 7.6 %copy-start.4 = (s32[144,512]{1,0:T(8,128)S(1)}, s32[144,512]{1,0:T(8,128)}, u32[]{:S(2)}) copy-start(s32[144,512]{1,0:T(8,128)} %ints.1) | copy-start | bytes 884740
  2.7 8.6 %collective-permute-start.1 = (f32[16,256]{1,0:T(8,128)S(1)}, f32[16,256]{1,0:T(8,128)S(1)}, u32[]{:S(2)}, u32[]{:S(2)}) collective-permute-start(f32[16,256]{1,0:T(8,128)S(1)} %get-tuple-element.39.after.refs_1_), channel_id=1, source_target_pairs={{0,1},{1,0},{2,3},{3,2},{4,5},{5,4},{6,7},{7,6},{8,9},{9,8},{10,11... | collective-permute-start | bytes 49160 | tf_op jit(solution)/shard_map/ppermute | solution.py:819
  5.8 5.5 %collective-permute-start = (f32[16,144]{1,0:T(8,128)S(1)}, f32[16,144]{1,0:T(8,128)S(1)}, u32[]{:S(2)}, u32[]{:S(2)}) collective-permute-start(f32[16,144]{1,0:T(8,128)S(1)} %get-tuple-element.42.refs_0_), channel_id=1, source_target_pairs={{0,3},{1,2},{2,1},{3,0},{4,7},{5,6},{6,5},{7,4},{8,11},{9,10},{10,... | collective-permute-start | bytes 27656 | tf_op jit(solution)/shard_map/ppermute | solution.py:829
  11.4 1.6 %collective-permute-start.3 = (f32[80,512]{1,0:T(8,128)S(1)}, f32[80,512]{1,0:T(8,128)S(1)}, u32[]{:S(2)}, u32[]{:S(2)}) collective-permute-start(f32[80,512]{1,0:T(8,128)S(1)} %get-tuple-element.57), channel_id=1, source_target_pairs={{0,8},{8,0},{16,24},{24,16},{1,9},{9,1},{17,25},{25,17},{2,10},{10... | collective-permute-start | bytes 491528 | tf_op jit(solution)/shard_map/ppermute | solution.py:819
  11.4 4.1 %collective-permute-start.2 = (f32[16,640]{1,0:T(8,128)S(1)}, f32[16,640]{1,0:T(8,128)S(1)}, u32[]{:S(2)}, u32[]{:S(2)}) collective-permute-start(f32[16,640]{1,0:T(8,128)S(1)} %get-tuple-element.48.after), channel_id=1, source_target_pairs={{0,4},{4,0},{1,5},{5,1},{2,6},{6,2},{3,7},{7,3},{8,12},{12,8},{9,1... | collective-permute-start | bytes 122888 | tf_op jit(solution)/shard_map/ppermute | solution.py:819
  13.0 5.8 %collective-permute-start.6 = (f32[32,512]{1,0:T(8,128)S(1)}, f32[32,512]{1,0:T(8,128)S(1)}, u32[]{:S(2)}, u32[]{:S(2)}) collective-permute-start(f32[32,512]{1,0:T(8,128)S(1)} %get-tuple-element.62.refs_0_), channel_id=1, source_target_pairs={{0,16},{8,24},{16,0},{24,8},{1,17},{9,25},{17,1},{25,9},{2,18},{10... | collective-permute-start | bytes 196616 | tf_op jit(solution)/shard_map/ppermute | solution.py:819
  14.6 4.3 %collective-permute-start.7 = (f32[32,512]{1,0:T(8,128)S(1)}, f32[32,512]{1,0:T(8,128)S(1)}, u32[]{:S(2)}, u32[]{:S(2)}) collective-permute-start(f32[32,512]{1,0:T(8,128)S(1)} %get-tuple-element.63.refs_1_), channel_id=1, source_target_pairs={{0,16},{8,24},{16,0},{24,8},{1,17},{9,25},{17,1},{25,9},{2,18},{10... | collective-permute-start | bytes 196616 | tf_op jit(solution)/shard_map/ppermute | solution.py:819
  15.8 3.0 %collective-permute-start.5 = (f32[8,512]{1,0:T(8,128)S(1)}, f32[8,512]{1,0:T(8,128)S(1)}, u32[]{:S(2)}, u32[]{:S(2)}) collective-permute-start(f32[8,512]{1,0:T(8,128)S(1)} %pad_maximum_fusion.b.a), channel_id=1, source_target_pairs={{0,8},{8,0},{16,24},{24,16},{1,9},{9,1},{17,25},{25,17},{2,10},{10... | collective-permute-start | bytes 49160 | tf_op jit(solution)/shard_map/ppermute | solution.py:819
  15.9 4.9 %collective-permute-start.4 = (f32[24,512]{1,0:T(8,128)S(1)}, f32[24,512]{1,0:T(8,128)S(1)}, u32[]{:S(2)}, u32[]{:S(2)}) collective-permute-start(f32[24,512]{1,0:T(8,128)S(1)} %stacked.1.tail), channel_id=1, source_target_pairs={{0,16},{8,24},{16,0},{24,8},{1,17},{9,25},{17,1},{25,9},{2,18},{10... | collective-permute-start | bytes 147464 | tf_op jit(solution)/shard_map/ppermute | solution.py:819
  17.5 3.2 %collective-permute-start.9 = (f32[8,512]{1,0:T(8,128)S(1)}, f32[8,512]{1,0:T(8,128)S(1)}, u32[]{:S(2)}, u32[]{:S(2)}) collective-permute-start(f32[8,512]{1,0:T(8,128)S(1)} %pad_maximum_fusion.b.a), channel_id=1, source_target_pairs={{0,24},{8,16},{16,8},{24,0},{1,25},{9,17},{17,9},{25,1},{2,26},{10... | collective-permute-start | bytes 49160 | tf_op jit(solution)/shard_map/ppermute | solution.py:819
  18.9 1.9 %collective-permute-start.8 = (f32[16,512]{1,0:T(8,128)S(1)}, f32[16,512]{1,0:T(8,128)S(1)}, u32[]{:S(2)}, u32[]{:S(2)}) collective-permute-start(f32[16,512]{1,0:T(8,128)S(1)} %get-tuple-element.64.refs_0_), channel_id=1, source_target_pairs={{0,8},{8,0},{16,24},{24,16},{1,9},{9,1},{17,25},{25,17},{2,10},{10... | collective-permute-start | bytes 98312 | tf_op jit(solution)/shard_map/ppermute | solution.py:819
  19.3 2.4 %collective-permute-start.10 = (f32[16,512]{1,0:T(8,128)S(1)}, f32[16,512]{1,0:T(8,128)S(1)}, u32[]{:S(2)}, u32[]{:S(2)}) collective-permute-start(f32[16,512]{1,0:T(8,128)S(1)} %get-tuple-element.67.refs_1_), channel_id=1, source_target_pairs={{0,8},{8,0},{16,24},{24,16},{1,9},{9,1},{17,25},{25,17},{2,10},{10... | collective-permute-start | bytes 98312 | tf_op jit(solution)/shard_map/ppermute | solution.py:819
  19.5 2.2 %collective-permute-start.11 = (f32[16,512]{1,0:T(8,128)S(1)}, f32[16,512]{1,0:T(8,128)S(1)}, u32[]{:S(2)}, u32[]{:S(2)}) collective-permute-start(f32[16,512]{1,0:T(8,128)S(1)} %get-tuple-element.68.refs_2_), channel_id=1, source_target_pairs={{0,8},{8,0},{16,24},{24,16},{1,9},{9,1},{17,25},{25,17},{2,10},{10... | collective-permute-start | bytes 98312 | tf_op jit(solution)/shard_map/ppermute | solution.py:819
  20.6 1.2 %collective-permute-start.12 = (f32[16,512]{1,0:T(8,128)S(1)}, f32[16,512]{1,0:T(8,128)S(1)}, u32[]{:S(2)}, u32[]{:S(2)}) collective-permute-start(f32[16,512]{1,0:T(8,128)S(1)} %get-tuple-element.69.refs_3_), channel_id=1, source_target_pairs={{0,8},{8,0},{16,24},{24,16},{1,9},{9,1},{17,25},{25,17},{2,10},{10... | collective-permute-start | bytes 98312 | tf_op jit(solution)/shard_map/ppermute | solution.py:819
where the time goes:
time: 23.5 us; the launch traced here: 23.4 us
  starting transfers between devices  12.2 us (52%)
  Pallas kernels  7.91 us (34%)
  waiting for transfers between devices  2.31 us (10%)
  between operations  0.81 us (3%)
    ppermute x12, starting transfers between devices, swapped(): lax.ppermute(x, axis, [(i, i ^ bit) for i in range(lax.axis_size(axis))])  9.72 us
    ppermute x1, starting transfers between devices, body(): lax.ppermute(m2, 'tx', [(i, (i - 1 if i % 2 == 0 else i + 1) % ntx) for i...  2.47 us
    pallas_call x1, Pallas kernels, first_sweep(): pl.pallas_call(first_kernel, out_shape=(pltpu.VMEM(e.shape, F32), half, h...  2.11 us
    pallas_call x1, Pallas kernels, pack_columns(): pl.pallas_call(pack_columns_kernel, out_shape=(pltpu.VMEM((MSG, rows), F3...  2.01 us
    pallas_call x1, Pallas kernels, other_half(): pl.pallas_call(other_kernel, out_shape=(jax.ShapeDtypeStruct(du.shape, F3...  1.49 us
    ppermute x12, waiting for transfers between devices, swapped(): lax.ppermute(x, axis, [(i, i ^ bit) for i in range(lax.axis_size(axis))])  1.49 us
    ppermute x1, waiting for transfers between devices, body(): lax.ppermute(m2, 'tx', [(i, (i - 1 if i % 2 == 0 else i + 1) % ntx) for i...  0.82 us
    pallas_call x1, Pallas kernels, prepare(): pl.pallas_call(prepare_kernel, out_shape=(plane, plane, plane), in_specs=...  0.78 us
  transfers between devices with their start and end apart: 13, of which 5 were waited for; matrix products, arithmetic and copies ran while one was open for 0% of the time, Pallas kernels for 18%

commit v1 on v0

--- a/solution.py
+++ b/solution.py
@@ -439,25 +439,12 @@
     return (z1r, z1i, d, coef_a, e1r, e1i), var
 
 
-def strips(rows, m2, m1, f2, f1, mn, ms, fn_ref, fs_ref):
-    kdev = 2
+def strip_lines(rows, m2, m1, f2, f1, mn, ms, fn_ref, fs_ref):
     width = mn.shape[1] - LANES
     pad = m1.shape[1]
-    ws = omegas(kdev)
     ty, count = lax.axis_index("ty"), lax.axis_size("ty")
-    first = (ty * rows).astype(F32)
-    total = rows * count
     fn = jnp.where(ty < count - 1, fn_ref[...], 0.0)
     fs = jnp.where(ty > 0, fs_ref[...], 0.0)
-
-    ay = AY
-    line = lax.broadcasted_iota(jnp.int32, (8, LANES), 0) // 2
-    out = []
-    for low, high, start in ((fs, ms[...], -2), (mn[...], fn, rows - 2)):
-        ax = metric((line + start).astype(F32) + first, total)
-        ax = jnp.concatenate([ax] * (low.shape[1] // LANES), axis=1)
-        out.append(strip_sweep(low, high, ws, ay, ax))
-
     mw, me = roles(m1[...], padded(m2[...], pad))
     fw, fe = roles(f1[...], padded(f2[...], pad))
     hi = rows - (pad - LANES)
@@ -472,23 +459,80 @@
 
     low_w, high_w = ended(fw, width, last), ended(mw, 0, 0)
     low_e, high_e = ended(me, width - LANES, last), ended(fe, width, 0)
+    return (fs, ms[...]), (mn[...], fn), (low_w, high_w), (low_e, high_e)
+
+
+def line_metric(lines, rows, width):
+    ax = metric((lines + lax.axis_index("ty") * rows).astype(F32), rows * lax.axis_size("ty"))
+    return jnp.concatenate([ax] * (width // LANES), axis=1)
+
+
+def column_metric(rows, pad):
+    first = (lax.axis_index("ty") * rows).astype(F32)
     row = lax.broadcasted_iota(jnp.int32, (8, pad), 1).astype(F32) + first
-    ax = metric(jnp.minimum(row, first + rows), total)
-    for low, high in ((low_w, high_w), (low_e, high_e)):
-        out.append(strip_sweep(low, high, ws, ax, ay))
-    return out
+    return metric(jnp.minimum(row, first + rows), rows * lax.axis_size("ty"))
+
+
+def strips(rows, *refs):
+    ws = omegas(2)
+    line = lax.broadcasted_iota(jnp.int32, (8, LANES), 0) // 2
+    south, north, west, east_ = strip_lines(rows, *refs)
+    width, pad = south[0].shape[1], west[0].shape[1]
+    out = [
+        strip_sweep(*pair, ws, AY, line_metric(line + start, rows, width))
+        for pair, start in ((south, -2), (north, rows - 2))
+    ]
+    ax = column_metric(rows, pad)
+    return out + [strip_sweep(*pair, ws, ax, AY) for pair in (west, east_)]
+
+
+def pair_variance(a, b, ws, g_across, g_along):
+    sides = (*a, *b)
+
+    def field(at):
+        return jnp.concatenate([x[at : at + 2] for x in sides], axis=0)
+
+    def single(at):
+        return jnp.concatenate([x[at : at + 1] for x in sides for _ in range(2)], axis=0)
+
+    zr, zi = field(0), field(2)
+    r, d, m = single(12), single(13), single(14)
+    w2 = 2.0 * strip_omega(zr.shape, ws)
+    up = lambda x: rolled(x, -2, 0)
+    nx = lambda x: rolled(x, -1, 1)
+    coef_a = (THETA * g_across * g_across) * (m * up(m) * (d + up(d)))
+    coef_l = (THETA * g_along * g_along) * (m * nx(m) * (d + nx(d)))
+    inner = face(zr, zi, up(zr), up(zi), r + up(r), coef_a, w2)
+    low_line = lax.rem(lax.broadcasted_iota(jnp.int32, zr.shape, 0) // 2, 2) == 0
+    sa = sl = None
+    along = face(zr, zi, nx(zr), nx(zi), r + nx(r), coef_l, w2)
+    for p in range(2):
+        outer = field(4 + 2 * p)
+        both = jnp.where(low_line, inner[p], outer) + jnp.where(low_line, outer, rolled(inner[p], 2, 0))
+        other = along[p] + rolled(along[p], 1, 1)
+        sa = both * both if sa is None else sa + both * both
+        sl = other * other if sl is None else sl + other * other
+    inv = recip(jnp.maximum(d, TINY_DEPTH))
+    ia = recip(THETA * g_across)
+    il = recip(THETA * g_along)
+    var = 0.125 * (ia * ia * sa + il * il * sl) * (inv * inv)
+    return var + rolled(var, -1, 0)
 
 
 def rim_kernel(rows, after, *refs):
     del after
     *refs, row_sums, col_sums = refs
-    width, pad = row_sums.shape[1], refs[1].shape[1]
-    for k, (_, var) in enumerate(strips(rows, *refs)):
-        for p in range(2):
-            if k < 2:
-                row_sums[2 * k + p, :] = var[2 + 2 * p, :width]
-            else:
-                col_sums[k - 2, p * pad : (p + 1) * pad] = var[2 + 2 * p, :]
+    ws = omegas(2)
+    south, north, west, east_ = strip_lines(rows, *refs)
+    width, pad = row_sums.shape[1], west[0].shape[1]
+    index = lax.broadcasted_iota(jnp.int32, (8, LANES), 0)
+    line = lax.rem(index // 2, 2) - 1 + index // 4 * rows
+    var = pair_variance(south, north, ws, AY, line_metric(line, rows, south[0].shape[1]))
+    for k in range(4):
+        row_sums[k, :] = var[2 * k, :width]
+    var = pair_variance(west, east_, ws, column_metric(rows, pad), AY)
+    for k in range(4):
+        col_sums[k // 2, k % 2 * pad : (k % 2 + 1) * pad] = var[2 * k, :]
     col_sums[2:, :] = jnp.zeros((2, width), F32)
 
 

time: 23.5 us -> 23.5 us (level)
  no operation moved by 1% of the time
where the time goes in v1:
time: 23.5 us; the launch traced here: 23.3 us
  starting transfers between devices  12.2 us (52%)
  Pallas kernels  7.87 us (33%)
  waiting for transfers between devices  2.34 us (10%)
  between operations  0.82 us (3%)
    ppermute x12, starting transfers between devices, swapped(): lax.ppermute(x, axis, [(i, i ^ bit) for i in range(lax.axis_size(axis))])  9.69 us
    ppermute x1, starting transfers between devices, body(): lax.ppermute(m2, 'tx', [(i, (i - 1 if i % 2 == 0 else i + 1) % ntx) for i...  2.47 us
    pallas_call x1, Pallas kernels, first_sweep(): pl.pallas_call(first_kernel, out_shape=(pltpu.VMEM(e.shape, F32), half, h...  2.11 us
    pallas_call x1, Pallas kernels, pack_columns(): pl.pallas_call(pack_columns_kernel, out_shape=(pltpu.VMEM((MSG, rows), F3...  2.01 us
    ppermute x12, waiting for transfers between devices, swapped(): lax.ppermute(x, axis, [(i, i ^ bit) for i in range(lax.axis_size(axis))])  1.52 us
    pallas_call x1, Pallas kernels, other_half(): pl.pallas_call(other_kernel, out_shape=(jax.ShapeDtypeStruct(du.shape, F3...  1.49 us
    ppermute x1, waiting for transfers between devices, body(): lax.ppermute(m2, 'tx', [(i, (i - 1 if i % 2 == 0 else i + 1) % ntx) for i...  0.82 us
    pallas_call x1, Pallas kernels, prepare(): pl.pallas_call(prepare_kernel, out_shape=(plane, plane, plane), in_specs=...  0.78 us
  transfers between devices with their start and end apart: 13, of which 5 were waited for; matrix products, arithmetic and copies ran while one was open for 0% of the time, Pallas kernels for 18%

profile of v1, /device:TPU:0, one launch (start us, length us, event | category | flops | bytes accessed | tf_op | source)
XLA Modules:
  0.0 23.3 jit_solution(4955885951824392903)
XLA Ops:
  0.6 0.0 copy-start.2
  0.6 0.0 copy-start
  0.7 0.0 copy-start.3
  0.7 0.0 copy-start.1
  0.7 0.0 copy-start.4
  0.7 2.0 %pack_columns.1 = (f32[16,144]{1,0:T(8,128)S(1)}, f32[16,256]{1,0:T(8,128)S(1)}) custom-call(f32[2,2,144,512]{3,2,1,0:T(8,128)} %e.3, f32[2,2,144,512]{3,2,1,0:T(8,128)} %q.5, f32[144,512]{1,0:T(8,128)} %d.7, s32[144,512]{1,0:T(8,128)} %ints.1, f32[144,512]{1,0:T(8,128)} %r.3), custom_call_target="tpu_custom_call" | custom-call | tf_op jit(solution)/shard_map/pack_columns/pallas_call | solution.py:126
  2.7 3.1 %collective-permute-start.1 = (f32[16,256]{1,0:T(8,128)S(1)}, f32[16,256]{1,0:T(8,128)S(1)}, u32[]{:S(2)}, u32[]{:S(2)}) collective-permute-start(f32[16,256]{1,0:T(8,128)S(1)} %get-tuple-element.39.after.refs_1_), channel_id=1, source_target_pairs={{0,1},{1,0},{2,3},{3,2},{4,5},{5,4},{6,7},{7,6},{8,9},{9,8},{10,11... | collective-permute-start | bytes 49160 | tf_op jit(solution)/shard_map/ppermute | solution.py:863
  5.8 2.5 %collective-permute-start = (f32[16,144]{1,0:T(8,128)S(1)}, f32[16,144]{1,0:T(8,128)S(1)}, u32[]{:S(2)}, u32[]{:S(2)}) collective-permute-start(f32[16,144]{1,0:T(8,128)S(1)} %get-tuple-element.42.refs_0_), channel_id=1, source_target_pairs={{0,3},{1,2},{2,1},{3,0},{4,7},{5,6},{6,5},{7,4},{8,11},{9,10},{10,... | collective-permute-start | bytes 27656 | tf_op jit(solution)/shard_map/ppermute | solution.py:873
  8.3 0.0 copy-done.2
  8.3 0.0 copy-done
  8.3 0.0 copy-done.3
  8.3 0.0 copy-done.1
  8.3 0.0 copy-done.4
  8.3 0.1 pack.1
  8.4 2.1 %first_sweep.1 = (f32[2,2,144,512]{3,2,1,0:T(8,128)S(1)}, f32[80,512]{1,0:T(8,128)S(1)}, f32[80,512]{1,0:T(8,128)S(1)}, f32[2,144,512]{2,1,0:T(8,128)S(1)}) custom-call(f32[2,2,144,512]{3,2,1,0:T(8,128)S(1)} %copy-done.1, f32[2,2,144,512]{3,2,1,0:T(8,128)S(1)} %copy-done, f32[144,512]{1,0:T(8,128)S(1)} %copy-done.2, ...), custom_call_target="tpu_custom_call" | custom-call | flops 23592960 | bytes 47185920 | tf_op jit(solution)/shard_map/first_sweep/pallas_call | solution.py:257
  10.5 0.8 %collective-permute-done.f2.refs_2_ = f32[16,144]{1,0:T(8,128)S(1)} collective-permute-done((f32[16,144]{1,0:T(8,128)S(1)}, f32[16,144]{1,0:T(8,128)S(1)}, u32[]{:S(2)}, u32[]{:S(2)}) %collective-permute-start) | collective-permute-done | bytes 9248 | tf_op jit(solution)/shard_map/ppermute | solution.py:873
  11.3 0.0 collective-permute-done.1.f1.refs_3_
  11.3 0.1 merge.1
  11.4 0.0 collective-permute-start.3
  11.4 1.6 %collective-permute-start.2 = (f32[16,640]{1,0:T(8,128)S(1)}, f32[16,640]{1,0:T(8,128)S(1)}, u32[]{:S(2)}, u32[]{:S(2)}) collective-permute-start(f32[16,640]{1,0:T(8,128)S(1)} %get-tuple-element.48.after), channel_id=1, source_target_pairs={{0,4},{4,0},{1,5},{5,1},{2,6},{6,2},{3,7},{7,3},{8,12},{12,8},{9,1... | collective-permute-start | bytes 122888 | tf_op jit(solution)/shard_map/ppermute | solution.py:863
  13.0 0.0 collective-permute-done.3.a
  13.0 1.6 %collective-permute-start.6 = (f32[32,512]{1,0:T(8,128)S(1)}, f32[32,512]{1,0:T(8,128)S(1)}, u32[]{:S(2)}, u32[]{:S(2)}) collective-permute-start(f32[32,512]{1,0:T(8,128)S(1)} %get-tuple-element.62.refs_0_), channel_id=1, source_target_pairs={{0,16},{8,24},{16,0},{24,8},{1,17},{9,25},{17,1},{25,9},{2,18},{10... | collective-permute-start | bytes 196616 | tf_op jit(solution)/shard_map/ppermute | solution.py:863
  14.6 0.5 %collective-permute-start.7 = (f32[32,512]{1,0:T(8,128)S(1)}, f32[32,512]{1,0:T(8,128)S(1)}, u32[]{:S(2)}, u32[]{:S(2)}) collective-permute-start(f32[32,512]{1,0:T(8,128)S(1)} %get-tuple-element.63.refs_1_), channel_id=1, source_target_pairs={{0,16},{8,24},{16,0},{24,8},{1,17},{9,25},{17,1},{25,9},{2,18},{10... | collective-permute-start | bytes 196616 | tf_op jit(solution)/shard_map/ppermute | solution.py:863
  15.1 0.4 %collective-permute-done.2.refs_6_.refs_7_ = f32[16,640]{1,0:T(8,128)S(1)} collective-permute-done((f32[16,640]{1,0:T(8,128)S(1)}, f32[16,640]{1,0:T(8,128)S(1)}, u32[]{:S(2)}, u32[]{:S(2)}) %collective-permute-start.2) | collective-permute-done | bytes 40992 | tf_op jit(solution)/shard_map/ppermute | solution.py:863
  15.5 0.2 %rim.1 = (f32[4,512]{1,0:T(4,128)S(1)}, f32[4,512]{1,0:T(4,128)S(1)}) custom-call(f32[16,512]{1,0:T(8,128)S(1)} %get-tuple-element.59.after.a, f32[16,144]{1,0:T(8,128)S(1)} %get-tuple-element.42.refs_0_, f32[16,256]{1,0:T(8,128)S(1)} %get-tuple-element.39.after.refs_1_, f32[16,144]{1,0:T(8,128)S(1)} %collective-permute-done.f2.refs_2_, ...), custom_call_target="tpu_custom_call" | custom-call | tf_op jit(solution)/shard_map/rim/pallas_call | solution.py:547
  15.8 0.1 collective-permute-start.5
  15.9 1.6 %collective-permute-start.4 = (f32[24,512]{1,0:T(8,128)S(1)}, f32[24,512]{1,0:T(8,128)S(1)}, u32[]{:S(2)}, u32[]{:S(2)}) collective-permute-start(f32[24,512]{1,0:T(8,128)S(1)} %stacked.1.tail), channel_id=1, source_target_pairs={{0,16},{8,24},{16,0},{24,8},{1,17},{9,25},{17,1},{25,9},{2,18},{10... | collective-permute-start | bytes 147464 | tf_op jit(solution)/shard_map/ppermute | solution.py:863
  17.5 0.3 %collective-permute-start.9 = (f32[8,512]{1,0:T(8,128)S(1)}, f32[8,512]{1,0:T(8,128)S(1)}, u32[]{:S(2)}, u32[]{:S(2)}) collective-permute-start(f32[8,512]{1,0:T(8,128)S(1)} %pad_maximum_fusion.b.a), channel_id=1, source_target_pairs={{0,24},{8,16},{16,8},{24,0},{1,25},{9,17},{17,9},{25,1},{2,26},{10... | collective-permute-start | bytes 49160 | tf_op jit(solution)/shard_map/ppermute | solution.py:863
  17.7 0.3 %held_strips.1 = (f32[48,640]{1,0:T(8,128)S(1)}, f32[48,640]{1,0:T(8,128)S(1)}, f32[48,256]{1,0:T(8,128)S(1)}, f32[48,256]{1,0:T(8,128)S(1)}) custom-call(f32[16,144]{1,0:T(8,128)S(1)} %get-tuple-element.42.refs_0_, f32[16,256]{1,0:T(8,128)S(1)} %get-tuple-element.39.after.refs_1_, f32[16,144]{1,0:T(8,128)S(1)} %collective-permute-done.f2.refs_2_, ...), custom_call_target="tpu_custom_call" | custom-call | tf_op jit(solution)/shard_map/held_strips/pallas_call | solution.py:576
  18.0 0.8 %prepare.1 = (f32[2,2,144,512]{3,2,1,0:T(8,128)S(1)}, f32[2,2,144,512]{3,2,1,0:T(8,128)S(1)}, f32[2,2,144,512]{3,2,1,0:T(8,128)S(1)}) custom-call(f32[2,2,144,512]{3,2,1,0:T(8,128)S(1)} %get-tuple-element.41.e1_in, f32[2,2,144,512]{3,2,1,0:T(8,128)S(1)} %copy-done, f32[144,512]{1,0:T(8,128)S(1)} %get-tuple-element.40.mask.m, ...), custom_call_target="tpu_custom_call" | custom-call | flops 11796480 | bytes 47185920 | tf_op jit(solution)/shard_map/prepare/pallas_call | solution.py:627
  18.8 0.0 collective-permute-done.5.b
  18.8 0.0 collective-permute-done.6.refs_2_
  18.8 0.1 collective-permute-done.7.refs_3_
  18.9 0.3 %collective-permute-start.8 = (f32[16,512]{1,0:T(8,128)S(1)}, f32[16,512]{1,0:T(8,128)S(1)}, u32[]{:S(2)}, u32[]{:S(2)}) collective-permute-start(f32[16,512]{1,0:T(8,128)S(1)} %get-tuple-element.64.refs_0_), channel_id=1, source_target_pairs={{0,8},{8,0},{16,24},{24,16},{1,9},{9,1},{17,25},{25,17},{2,10},{10... | collective-permute-start | bytes 98312 | tf_op jit(solution)/shard_map/ppermute | solution.py:863
  19.3 0.2 collective-permute-start.10
  19.5 0.3 %collective-permute-start.11 = (f32[16,512]{1,0:T(8,128)S(1)}, f32[16,512]{1,0:T(8,128)S(1)}, u32[]{:S(2)}, u32[]{:S(2)}) collective-permute-start(f32[16,512]{1,0:T(8,128)S(1)} %get-tuple-element.68.refs_2_), channel_id=1, source_target_pairs={{0,8},{8,0},{16,24},{24,16},{1,9},{9,1},{17,25},{25,17},{2,10},{10... | collective-permute-start | bytes 98312 | tf_op jit(solution)/shard_map/ppermute | solution.py:863
  19.8 0.8 %collective-permute-done.9.refs_0_ = f32[8,512]{1,0:T(8,128)S(1)} collective-permute-done((f32[8,512]{1,0:T(8,128)S(1)}, f32[8,512]{1,0:T(8,128)S(1)}, u32[]{:S(2)}, u32[]{:S(2)}) %collective-permute-start.9) | collective-permute-done | bytes 16416 | tf_op jit(solution)/shard_map/ppermute | solution.py:863
  20.6 0.2 collective-permute-start.12
  20.8 0.0 collective-permute-done.4.partner
  20.8 0.0 collective-permute-done.8.after.refs_0_
  20.8 0.7 %own_half.1 = (f32[2,2,72,512]{3,2,1,0:T(8,128)S(1)}, f32[2,2,72,512]{3,2,1,0:T(8,128)S(1)}, f32[72,512]{1,0:T(8,128)S(1)}, f32[8,512]{1,0:T(8,128)S(1)}, f32[8,512]{1,0:T(8,128)S(1)}, /*index=5*/f32[256,128]{1,0:T(8,128)S(1)}) custom-call(f32[2,2,144,512]{3,2,1,0:T(8,128)S(1)} %get-tuple-element.53.du, f32[2,2,144,512]{3,2,1,0:T(8,128)S(1)} %get-tuple-element.54.dv, ...), custom_call_target="tpu_custom_call" | custom-call | tf_op jit(solution)/shard_map/own_half/pallas_call | solution.py:757
  21.5 0.1 sub.3.eta_own
  21.6 0.0 collective-permute-done.10.refs_1_
  21.6 0.0 collective-permute-done.11.refs_2_
  21.6 0.2 collective-permute-done.12.refs_3_
  21.8 1.5 %other_half.1 = (f32[2,2,144,512]{3,2,1,0:T(8,128)}, f32[144,512]{1,0:T(8,128)}) custom-call(f32[2,2,144,512]{3,2,1,0:T(8,128)S(1)} %get-tuple-element.53.du, f32[2,2,144,512]{3,2,1,0:T(8,128)S(1)} %get-tuple-element.54.dv, f32[2,2,144,512]{3,2,1,0:T(8,128)S(1)} %get-tuple-element.55.refs_0_.base, f32[2,144,512]{2,1,0:T(8,128)S(1)} %get-tuple-element.56.coef, ...), custom_call_target="tpu_custom_call" | custom-call | tf_op jit(solution)/shard_map/other_half/pallas_call | solution.py:846
  (6 shorter events, 0.1 us)
Async XLA Ops:
  0.6 7.6 %copy-start.2 = (f32[144,512]{1,0:T(8,128)S(1)}, f32[144,512]{1,0:T(8,128)}, u32[]{:S(2)}) copy-start(f32[144,512]{1,0:T(8,128)} %d.7) | copy-start | bytes 884740
  0.6 7.6 %copy-start = (f32[2,2,144,512]{3,2,1,0:T(8,128)S(1)}, f32[2,2,144,512]{3,2,1,0:T(8,128)}, u32[]{:S(2)}) copy-start(f32[2,2,144,512]{3,2,1,0:T(8,128)} %q.5) | copy-start | bytes 3538948
  0.7 7.6 %copy-start.3 = (f32[144,512]{1,0:T(8,128)S(1)}, f32[144,512]{1,0:T(8,128)}, u32[]{:S(2)}) copy-start(f32[144,512]{1,0:T(8,128)} %r.3) | copy-start | bytes 884740
  0.7 7.6 %copy-start.1 = (f32[2,2,144,512]{3,2,1,0:T(8,128)S(1)}, f32[2,2,144,512]{3,2,1,0:T(8,128)}, u32[]{:S(2)}) copy-start(f32[2,2,144,512]{3,2,1,0:T(8,128)} %e.3) | copy-start | bytes 3538948
  0.7 7.6 %copy-start.4 = (s32[144,512]{1,0:T(8,128)S(1)}, s32[144,512]{1,0:T(8,128)}, u32[]{:S(2)}) copy-start(s32[144,512]{1,0:T(8,128)} %ints.1) | copy-start | bytes 884740
  2.7 8.6 %collective-permute-start.1 = (f32[16,256]{1,0:T(8,128)S(1)}, f32[16,256]{1,0:T(8,128)S(1)}, u32[]{:S(2)}, u32[]{:S(2)}) collective-permute-start(f32[16,256]{1,0:T(8,128)S(1)} %get-tuple-element.39.after.refs_1_), channel_id=1, source_target_pairs={{0,1},{1,0},{2,3},{3,2},{4,5},{5,4},{6,7},{7,6},{8,9},{9,8},{10,11... | collective-permute-start | bytes 49160 | tf_op jit(solution)/shard_map/ppermute | solution.py:863
  5.8 5.5 %collective-permute-start = (f32[16,144]{1,0:T(8,128)S(1)}, f32[16,144]{1,0:T(8,128)S(1)}, u32[]{:S(2)}, u32[]{:S(2)}) collective-permute-start(f32[16,144]{1,0:T(8,128)S(1)} %get-tuple-element.42.refs_0_), channel_id=1, source_target_pairs={{0,3},{1,2},{2,1},{3,0},{4,7},{5,6},{6,5},{7,4},{8,11},{9,10},{10,... | collective-permute-start | bytes 27656 | tf_op jit(solution)/shard_map/ppermute | solution.py:873
  11.4 1.6 %collective-permute-start.3 = (f32[80,512]{1,0:T(8,128)S(1)}, f32[80,512]{1,0:T(8,128)S(1)}, u32[]{:S(2)}, u32[]{:S(2)}) collective-permute-start(f32[80,512]{1,0:T(8,128)S(1)} %get-tuple-element.57), channel_id=1, source_target_pairs={{0,8},{8,0},{16,24},{24,16},{1,9},{9,1},{17,25},{25,17},{2,10},{10... | collective-permute-start | bytes 491528 | tf_op jit(solution)/shard_map/ppermute | solution.py:863
  11.4 4.1 %collective-permute-start.2 = (f32[16,640]{1,0:T(8,128)S(1)}, f32[16,640]{1,0:T(8,128)S(1)}, u32[]{:S(2)}, u32[]{:S(2)}) collective-permute-start(f32[16,640]{1,0:T(8,128)S(1)} %get-tuple-element.48.after), channel_id=1, source_target_pairs={{0,4},{4,0},{1,5},{5,1},{2,6},{6,2},{3,7},{7,3},{8,12},{12,8},{9,1... | collective-permute-start | bytes 122888 | tf_op jit(solution)/shard_map/ppermute | solution.py:863
  13.0 5.8 %collective-permute-start.6 = (f32[32,512]{1,0:T(8,128)S(1)}, f32[32,512]{1,0:T(8,128)S(1)}, u32[]{:S(2)}, u32[]{:S(2)}) collective-permute-start(f32[32,512]{1,0:T(8,128)S(1)} %get-tuple-element.62.refs_0_), channel_id=1, source_target_pairs={{0,16},{8,24},{16,0},{24,8},{1,17},{9,25},{17,1},{25,9},{2,18},{10... | collective-permute-start | bytes 196616 | tf_op jit(solution)/shard_map/ppermute | solution.py:863
  14.6 4.3 %collective-permute-start.7 = (f32[32,512]{1,0:T(8,128)S(1)}, f32[32,512]{1,0:T(8,128)S(1)}, u32[]{:S(2)}, u32[]{:S(2)}) collective-permute-start(f32[32,512]{1,0:T(8,128)S(1)} %get-tuple-element.63.refs_1_), channel_id=1, source_target_pairs={{0,16},{8,24},{16,0},{24,8},{1,17},{9,25},{17,1},{25,9},{2,18},{10... | collective-permute-start | bytes 196616 | tf_op jit(solution)/shard_map/ppermute | solution.py:863
  15.8 3.0 %collective-permute-start.5 = (f32[8,512]{1,0:T(8,128)S(1)}, f32[8,512]{1,0:T(8,128)S(1)}, u32[]{:S(2)}, u32[]{:S(2)}) collective-permute-start(f32[8,512]{1,0:T(8,128)S(1)} %pad_maximum_fusion.b.a), channel_id=1, source_target_pairs={{0,8},{8,0},{16,24},{24,16},{1,9},{9,1},{17,25},{25,17},{2,10},{10... | collective-permute-start | bytes 49160 | tf_op jit(solution)/shard_map/ppermute | solution.py:863
  15.9 4.9 %collective-permute-start.4 = (f32[24,512]{1,0:T(8,128)S(1)}, f32[24,512]{1,0:T(8,128)S(1)}, u32[]{:S(2)}, u32[]{:S(2)}) collective-permute-start(f32[24,512]{1,0:T(8,128)S(1)} %stacked.1.tail), channel_id=1, source_target_pairs={{0,16},{8,24},{16,0},{24,8},{1,17},{9,25},{17,1},{25,9},{2,18},{10... | collective-permute-start | bytes 147464 | tf_op jit(solution)/shard_map/ppermute | solution.py:863
  17.5 3.2 %collective-permute-start.9 = (f32[8,512]{1,0:T(8,128)S(1)}, f32[8,512]{1,0:T(8,128)S(1)}, u32[]{:S(2)}, u32[]{:S(2)}) collective-permute-start(f32[8,512]{1,0:T(8,128)S(1)} %pad_maximum_fusion.b.a), channel_id=1, source_target_pairs={{0,24},{8,16},{16,8},{24,0},{1,25},{9,17},{17,9},{25,1},{2,26},{10... | collective-permute-start | bytes 49160 | tf_op jit(solution)/shard_map/ppermute | solution.py:863
  18.9 1.9 %collective-permute-start.8 = (f32[16,512]{1,0:T(8,128)S(1)}, f32[16,512]{1,0:T(8,128)S(1)}, u32[]{:S(2)}, u32[]{:S(2)}) collective-permute-start(f32[16,512]{1,0:T(8,128)S(1)} %get-tuple-element.64.refs_0_), channel_id=1, source_target_pairs={{0,8},{8,0},{16,24},{24,16},{1,9},{9,1},{17,25},{25,17},{2,10},{10... | collective-permute-start | bytes 98312 | tf_op jit(solution)/shard_map/ppermute | solution.py:863
  19.3 2.4 %collective-permute-start.10 = (f32[16,512]{1,0:T(8,128)S(1)}, f32[16,512]{1,0:T(8,128)S(1)}, u32[]{:S(2)}, u32[]{:S(2)}) collective-permute-start(f32[16,512]{1,0:T(8,128)S(1)} %get-tuple-element.67.refs_1_), channel_id=1, source_target_pairs={{0,8},{8,0},{16,24},{24,16},{1,9},{9,1},{17,25},{25,17},{2,10},{10... | collective-permute-start | bytes 98312 | tf_op jit(solution)/shard_map/ppermute | solution.py:863
  19.5 2.1 %collective-permute-start.11 = (f32[16,512]{1,0:T(8,128)S(1)}, f32[16,512]{1,0:T(8,128)S(1)}, u32[]{:S(2)}, u32[]{:S(2)}) collective-permute-start(f32[16,512]{1,0:T(8,128)S(1)} %get-tuple-element.68.refs_2_), channel_id=1, source_target_pairs={{0,8},{8,0},{16,24},{24,16},{1,9},{9,1},{17,25},{25,17},{2,10},{10... | collective-permute-start | bytes 98312 | tf_op jit(solution)/shard_map/ppermute | solution.py:863
  20.6 1.2 %collective-permute-start.12 = (f32[16,512]{1,0:T(8,128)S(1)}, f32[16,512]{1,0:T(8,128)S(1)}, u32[]{:S(2)}, u32[]{:S(2)}) collective-permute-start(f32[16,512]{1,0:T(8,128)S(1)} %get-tuple-element.69.refs_3_), channel_id=1, source_target_pairs={{0,8},{8,0},{16,24},{24,16},{1,9},{9,1},{17,25},{25,17},{2,10},{10... | collective-permute-start | bytes 98312 | tf_op jit(solution)/shard_map/ppermute | solution.py:863

commit v2 on v1

--- a/solution.py
+++ b/solution.py
@@ -201,7 +201,7 @@
 def first_kernel(e, q, d, mask, r, after, e1, send, keep, coef, var):
     del after
     kdev, _, rows, width = e.shape
-    size = 16
+    size = 24
     ws = omegas(kdev)
     last_v = [jnp.zeros((1, width), F32)] * (2 * kdev)
     for at in range(0, rows, size):
@@ -585,7 +585,7 @@
 
 def prepare_kernel(e1_in, q, m, ss, sn, sw, se, du, dv, base, e1, cols):
     kdev, _, rows, width = e1_in.shape
-    size = 16
+    size = 24
     ws = omegas(kdev)
     e1[...] = e1_in[...]
     for p in range(2):

time: 23.5 us -> 23.5 us (level)
  no operation moved by 1% of the time
where the time goes in v2:
time: 23.5 us; the launch traced here: 23.3 us
  starting transfers between devices  12.1 us (51%)
  Pallas kernels  7.68 us (33%)
  waiting for transfers between devices  2.54 us (11%)
  between operations  0.82 us (3%)
    ppermute x12, starting transfers between devices, swapped(): lax.ppermute(x, axis, [(i, i ^ bit) for i in range(lax.axis_size(axis))])  9.67 us
    ppermute x1, starting transfers between devices, body(): lax.ppermute(m2, 'tx', [(i, (i - 1 if i % 2 == 0 else i + 1) % ntx) for i...  2.47 us
    pallas_call x1, Pallas kernels, pack_columns(): pl.pallas_call(pack_columns_kernel, out_shape=(pltpu.VMEM((MSG, rows), F3...  2.01 us
    pallas_call x1, Pallas kernels, first_sweep(): pl.pallas_call(first_kernel, out_shape=(pltpu.VMEM(e.shape, F32), half, h...  1.94 us
    ppermute x12, waiting for transfers between devices, swapped(): lax.ppermute(x, axis, [(i, i ^ bit) for i in range(lax.axis_size(axis))])  1.55 us
    pallas_call x1, Pallas kernels, other_half(): pl.pallas_call(other_kernel, out_shape=(jax.ShapeDtypeStruct(du.shape, F3...  1.49 us
    ppermute x1, waiting for transfers between devices, body(): lax.ppermute(m2, 'tx', [(i, (i - 1 if i % 2 == 0 else i + 1) % ntx) for i...  0.99 us
    pallas_call x1, Pallas kernels, prepare(): pl.pallas_call(prepare_kernel, out_shape=(plane, plane, plane), in_specs=...  0.76 us
  transfers between devices with their start and end apart: 13, of which 5 were waited for; matrix products, arithmetic and copies ran while one was open for 0% of the time, Pallas kernels for 18%

profile of v2, /device:TPU:0, one launch (start us, length us, event | category | flops | bytes accessed | tf_op | source)
XLA Modules:
  0.0 23.3 jit_solution(17570453939570422733)
XLA Ops:
  0.6 0.0 copy-start.2
  0.6 0.0 copy-start
  0.7 0.0 copy-start.3
  0.7 0.0 copy-start.1
  0.7 0.0 copy-start.4
  0.7 2.0 %pack_columns.1 = (f32[16,144]{1,0:T(8,128)S(1)}, f32[16,256]{1,0:T(8,128)S(1)}) custom-call(f32[2,2,144,512]{3,2,1,0:T(8,128)} %e.3, f32[2,2,144,512]{3,2,1,0:T(8,128)} %q.5, f32[144,512]{1,0:T(8,128)} %d.7, s32[144,512]{1,0:T(8,128)} %ints.1, f32[144,512]{1,0:T(8,128)} %r.3), custom_call_target="tpu_custom_call" | custom-call | tf_op jit(solution)/shard_map/pack_columns/pallas_call | solution.py:126
  2.7 3.1 %collective-permute-start.1 = (f32[16,256]{1,0:T(8,128)S(1)}, f32[16,256]{1,0:T(8,128)S(1)}, u32[]{:S(2)}, u32[]{:S(2)}) collective-permute-start(f32[16,256]{1,0:T(8,128)S(1)} %get-tuple-element.39.after.refs_1_), channel_id=1, source_target_pairs={{0,1},{1,0},{2,3},{3,2},{4,5},{5,4},{6,7},{7,6},{8,9},{9,8},{10,11... | collective-permute-start | bytes 49160 | tf_op jit(solution)/shard_map/ppermute | solution.py:863
  5.8 2.5 %collective-permute-start = (f32[16,144]{1,0:T(8,128)S(1)}, f32[16,144]{1,0:T(8,128)S(1)}, u32[]{:S(2)}, u32[]{:S(2)}) collective-permute-start(f32[16,144]{1,0:T(8,128)S(1)} %get-tuple-element.42.refs_0_), channel_id=1, source_target_pairs={{0,3},{1,2},{2,1},{3,0},{4,7},{5,6},{6,5},{7,4},{8,11},{9,10},{10,... | collective-permute-start | bytes 27656 | tf_op jit(solution)/shard_map/ppermute | solution.py:873
  8.3 0.0 copy-done.2
  8.3 0.0 copy-done
  8.3 0.0 copy-done.3
  8.3 0.0 copy-done.1
  8.3 0.0 copy-done.4
  8.3 0.1 pack.1
  8.4 1.9 %first_sweep.1 = (f32[2,2,144,512]{3,2,1,0:T(8,128)S(1)}, f32[80,512]{1,0:T(8,128)S(1)}, f32[80,512]{1,0:T(8,128)S(1)}, f32[2,144,512]{2,1,0:T(8,128)S(1)}) custom-call(f32[2,2,144,512]{3,2,1,0:T(8,128)S(1)} %copy-done.1, f32[2,2,144,512]{3,2,1,0:T(8,128)S(1)} %copy-done, f32[144,512]{1,0:T(8,128)S(1)} %copy-done.2, ...), custom_call_target="tpu_custom_call" | custom-call | flops 23592960 | bytes 47185920 | tf_op jit(solution)/shard_map/first_sweep/pallas_call | solution.py:257
  10.3 1.0 %collective-permute-done.f2.refs_2_ = f32[16,144]{1,0:T(8,128)S(1)} collective-permute-done((f32[16,144]{1,0:T(8,128)S(1)}, f32[16,144]{1,0:T(8,128)S(1)}, u32[]{:S(2)}, u32[]{:S(2)}) %collective-permute-start) | collective-permute-done | bytes 9248 | tf_op jit(solution)/shard_map/ppermute | solution.py:873
  11.3 0.0 collective-permute-done.1.f1.refs_3_
  11.3 0.1 merge.1
  11.4 0.0 collective-permute-start.3
  11.4 1.6 %collective-permute-start.2 = (f32[16,640]{1,0:T(8,128)S(1)}, f32[16,640]{1,0:T(8,128)S(1)}, u32[]{:S(2)}, u32[]{:S(2)}) collective-permute-start(f32[16,640]{1,0:T(8,128)S(1)} %get-tuple-element.48.after), channel_id=1, source_target_pairs={{0,4},{4,0},{1,5},{5,1},{2,6},{6,2},{3,7},{7,3},{8,12},{12,8},{9,1... | collective-permute-start | bytes 122888 | tf_op jit(solution)/shard_map/ppermute | solution.py:863
  13.0 0.0 collective-permute-done.3.a
  13.0 1.6 %collective-permute-start.6 = (f32[32,512]{1,0:T(8,128)S(1)}, f32[32,512]{1,0:T(8,128)S(1)}, u32[]{:S(2)}, u32[]{:S(2)}) collective-permute-start(f32[32,512]{1,0:T(8,128)S(1)} %get-tuple-element.62.refs_0_), channel_id=1, source_target_pairs={{0,16},{8,24},{16,0},{24,8},{1,17},{9,25},{17,1},{25,9},{2,18},{10... | collective-permute-start | bytes 196616 | tf_op jit(solution)/shard_map/ppermute | solution.py:863
  14.6 0.5 %collective-permute-start.7 = (f32[32,512]{1,0:T(8,128)S(1)}, f32[32,512]{1,0:T(8,128)S(1)}, u32[]{:S(2)}, u32[]{:S(2)}) collective-permute-start(f32[32,512]{1,0:T(8,128)S(1)} %get-tuple-element.63.refs_1_), channel_id=1, source_target_pairs={{0,16},{8,24},{16,0},{24,8},{1,17},{9,25},{17,1},{25,9},{2,18},{10... | collective-permute-start | bytes 196616 | tf_op jit(solution)/shard_map/ppermute | solution.py:863
  15.1 0.4 %collective-permute-done.2.refs_6_.refs_7_ = f32[16,640]{1,0:T(8,128)S(1)} collective-permute-done((f32[16,640]{1,0:T(8,128)S(1)}, f32[16,640]{1,0:T(8,128)S(1)}, u32[]{:S(2)}, u32[]{:S(2)}) %collective-permute-start.2) | collective-permute-done | bytes 40992 | tf_op jit(solution)/shard_map/ppermute | solution.py:863
  15.5 0.2 %rim.1 = (f32[4,512]{1,0:T(4,128)S(1)}, f32[4,512]{1,0:T(4,128)S(1)}) custom-call(f32[16,512]{1,0:T(8,128)S(1)} %get-tuple-element.59.after.a, f32[16,144]{1,0:T(8,128)S(1)} %get-tuple-element.42.refs_0_, f32[16,256]{1,0:T(8,128)S(1)} %get-tuple-element.39.after.refs_1_, f32[16,144]{1,0:T(8,128)S(1)} %collective-permute-done.f2.refs_2_, ...), custom_call_target="tpu_custom_call" | custom-call | tf_op jit(solution)/shard_map/rim/pallas_call | solution.py:547
  15.8 0.1 collective-permute-start.5
  15.9 1.6 %collective-permute-start.4 = (f32[24,512]{1,0:T(8,128)S(1)}, f32[24,512]{1,0:T(8,128)S(1)}, u32[]{:S(2)}, u32[]{:S(2)}) collective-permute-start(f32[24,512]{1,0:T(8,128)S(1)} %stacked.1.tail), channel_id=1, source_target_pairs={{0,16},{8,24},{16,0},{24,8},{1,17},{9,25},{17,1},{25,9},{2,18},{10... | collective-permute-start | bytes 147464 | tf_op jit(solution)/shard_map/ppermute | solution.py:863
  17.5 0.3 %collective-permute-start.9 = (f32[8,512]{1,0:T(8,128)S(1)}, f32[8,512]{1,0:T(8,128)S(1)}, u32[]{:S(2)}, u32[]{:S(2)}) collective-permute-start(f32[8,512]{1,0:T(8,128)S(1)} %pad_maximum_fusion.b.a), channel_id=1, source_target_pairs={{0,24},{8,16},{16,8},{24,0},{1,25},{9,17},{17,9},{25,1},{2,26},{10... | collective-permute-start | bytes 49160 | tf_op jit(solution)/shard_map/ppermute | solution.py:863
  17.7 0.3 %held_strips.1 = (f32[48,640]{1,0:T(8,128)S(1)}, f32[48,640]{1,0:T(8,128)S(1)}, f32[48,256]{1,0:T(8,128)S(1)}, f32[48,256]{1,0:T(8,128)S(1)}) custom-call(f32[16,144]{1,0:T(8,128)S(1)} %get-tuple-element.42.refs_0_, f32[16,256]{1,0:T(8,128)S(1)} %get-tuple-element.39.after.refs_1_, f32[16,144]{1,0:T(8,128)S(1)} %collective-permute-done.f2.refs_2_, ...), custom_call_target="tpu_custom_call" | custom-call | tf_op jit(solution)/shard_map/held_strips/pallas_call | solution.py:576
  18.0 0.8 %prepare.1 = (f32[2,2,144,512]{3,2,1,0:T(8,128)S(1)}, f32[2,2,144,512]{3,2,1,0:T(8,128)S(1)}, f32[2,2,144,512]{3,2,1,0:T(8,128)S(1)}) custom-call(f32[2,2,144,512]{3,2,1,0:T(8,128)S(1)} %get-tuple-element.41.e1_in, f32[2,2,144,512]{3,2,1,0:T(8,128)S(1)} %copy-done, f32[144,512]{1,0:T(8,128)S(1)} %get-tuple-element.40.mask.m, ...), custom_call_target="tpu_custom_call" | custom-call | flops 11796480 | bytes 47185920 | tf_op jit(solution)/shard_map/prepare/pallas_call | solution.py:627
  18.8 0.0 collective-permute-done.5.b
  18.8 0.0 collective-permute-done.6.refs_2_
  18.8 0.1 collective-permute-done.7.refs_3_
  18.9 0.3 %collective-permute-start.8 = (f32[16,512]{1,0:T(8,128)S(1)}, f32[16,512]{1,0:T(8,128)S(1)}, u32[]{:S(2)}, u32[]{:S(2)}) collective-permute-start(f32[16,512]{1,0:T(8,128)S(1)} %get-tuple-element.64.refs_0_), channel_id=1, source_target_pairs={{0,8},{8,0},{16,24},{24,16},{1,9},{9,1},{17,25},{25,17},{2,10},{10... | collective-permute-start | bytes 98312 | tf_op jit(solution)/shard_map/ppermute | solution.py:863
  19.3 0.2 %collective-permute-start.10 = (f32[16,512]{1,0:T(8,128)S(1)}, f32[16,512]{1,0:T(8,128)S(1)}, u32[]{:S(2)}, u32[]{:S(2)}) collective-permute-start(f32[16,512]{1,0:T(8,128)S(1)} %get-tuple-element.67.refs_1_), channel_id=1, source_target_pairs={{0,8},{8,0},{16,24},{24,16},{1,9},{9,1},{17,25},{25,17},{2,10},{10... | collective-permute-start | bytes 98312 | tf_op jit(solution)/shard_map/ppermute | solution.py:863
  19.5 0.3 %collective-permute-start.11 = (f32[16,512]{1,0:T(8,128)S(1)}, f32[16,512]{1,0:T(8,128)S(1)}, u32[]{:S(2)}, u32[]{:S(2)}) collective-permute-start(f32[16,512]{1,0:T(8,128)S(1)} %get-tuple-element.68.refs_2_), channel_id=1, source_target_pairs={{0,8},{8,0},{16,24},{24,16},{1,9},{9,1},{17,25},{25,17},{2,10},{10... | collective-permute-start | bytes 98312 | tf_op jit(solution)/shard_map/ppermute | solution.py:863
  19.8 0.9 %collective-permute-done.9.refs_0_ = f32[8,512]{1,0:T(8,128)S(1)} collective-permute-done((f32[8,512]{1,0:T(8,128)S(1)}, f32[8,512]{1,0:T(8,128)S(1)}, u32[]{:S(2)}, u32[]{:S(2)}) %collective-permute-start.9) | collective-permute-done | bytes 16416 | tf_op jit(solution)/shard_map/ppermute | solution.py:863
  20.6 0.2 collective-permute-start.12
  20.8 0.0 collective-permute-done.4.partner
  20.8 0.0 collective-permute-done.8.after.refs_0_
  20.8 0.7 %own_half.1 = (f32[2,2,72,512]{3,2,1,0:T(8,128)S(1)}, f32[2,2,72,512]{3,2,1,0:T(8,128)S(1)}, f32[72,512]{1,0:T(8,128)S(1)}, f32[8,512]{1,0:T(8,128)S(1)}, f32[8,512]{1,0:T(8,128)S(1)}, /*index=5*/f32[256,128]{1,0:T(8,128)S(1)}) custom-call(f32[2,2,144,512]{3,2,1,0:T(8,128)S(1)} %get-tuple-element.53.du, f32[2,2,144,512]{3,2,1,0:T(8,128)S(1)} %get-tuple-element.54.dv, ...), custom_call_target="tpu_custom_call" | custom-call | tf_op jit(solution)/shard_map/own_half/pallas_call | solution.py:757
  21.5 0.1 sub.3.eta_own
  21.6 0.0 collective-permute-done.10.refs_1_
  21.6 0.0 collective-permute-done.11.refs_2_
  21.6 0.2 collective-permute-done.12.refs_3_
  21.8 1.5 %other_half.1 = (f32[2,2,144,512]{3,2,1,0:T(8,128)}, f32[144,512]{1,0:T(8,128)}) custom-call(f32[2,2,144,512]{3,2,1,0:T(8,128)S(1)} %get-tuple-element.53.du, f32[2,2,144,512]{3,2,1,0:T(8,128)S(1)} %get-tuple-element.54.dv, f32[2,2,144,512]{3,2,1,0:T(8,128)S(1)} %get-tuple-element.55.refs_0_.base, f32[2,144,512]{2,1,0:T(8,128)S(1)} %get-tuple-element.56.coef, ...), custom_call_target="tpu_custom_call" | custom-call | tf_op jit(solution)/shard_map/other_half/pallas_call | solution.py:846
  (6 shorter events, 0.1 us)
Async XLA Ops:
  0.6 7.6 %copy-start.2 = (f32[144,512]{1,0:T(8,128)S(1)}, f32[144,512]{1,0:T(8,128)}, u32[]{:S(2)}) copy-start(f32[144,512]{1,0:T(8,128)} %d.7) | copy-start | bytes 884740
  0.6 7.6 %copy-start = (f32[2,2,144,512]{3,2,1,0:T(8,128)S(1)}, f32[2,2,144,512]{3,2,1,0:T(8,128)}, u32[]{:S(2)}) copy-start(f32[2,2,144,512]{3,2,1,0:T(8,128)} %q.5) | copy-start | bytes 3538948
  0.7 7.6 %copy-start.3 = (f32[144,512]{1,0:T(8,128)S(1)}, f32[144,512]{1,0:T(8,128)}, u32[]{:S(2)}) copy-start(f32[144,512]{1,0:T(8,128)} %r.3) | copy-start | bytes 884740
  0.7 7.6 %copy-start.1 = (f32[2,2,144,512]{3,2,1,0:T(8,128)S(1)}, f32[2,2,144,512]{3,2,1,0:T(8,128)}, u32[]{:S(2)}) copy-start(f32[2,2,144,512]{3,2,1,0:T(8,128)} %e.3) | copy-start | bytes 3538948
  0.7 7.6 %copy-start.4 = (s32[144,512]{1,0:T(8,128)S(1)}, s32[144,512]{1,0:T(8,128)}, u32[]{:S(2)}) copy-start(s32[144,512]{1,0:T(8,128)} %ints.1) | copy-start | bytes 884740
  2.7 8.6 %collective-permute-start.1 = (f32[16,256]{1,0:T(8,128)S(1)}, f32[16,256]{1,0:T(8,128)S(1)}, u32[]{:S(2)}, u32[]{:S(2)}) collective-permute-start(f32[16,256]{1,0:T(8,128)S(1)} %get-tuple-element.39.after.refs_1_), channel_id=1, source_target_pairs={{0,1},{1,0},{2,3},{3,2},{4,5},{5,4},{6,7},{7,6},{8,9},{9,8},{10,11... | collective-permute-start | bytes 49160 | tf_op jit(solution)/shard_map/ppermute | solution.py:863
  5.8 5.5 %collective-permute-start = (f32[16,144]{1,0:T(8,128)S(1)}, f32[16,144]{1,0:T(8,128)S(1)}, u32[]{:S(2)}, u32[]{:S(2)}) collective-permute-start(f32[16,144]{1,0:T(8,128)S(1)} %get-tuple-element.42.refs_0_), channel_id=1, source_target_pairs={{0,3},{1,2},{2,1},{3,0},{4,7},{5,6},{6,5},{7,4},{8,11},{9,10},{10,... | collective-permute-start | bytes 27656 | tf_op jit(solution)/shard_map/ppermute | solution.py:873
  11.4 1.6 %collective-permute-start.3 = (f32[80,512]{1,0:T(8,128)S(1)}, f32[80,512]{1,0:T(8,128)S(1)}, u32[]{:S(2)}, u32[]{:S(2)}) collective-permute-start(f32[80,512]{1,0:T(8,128)S(1)} %get-tuple-element.57), channel_id=1, source_target_pairs={{0,8},{8,0},{16,24},{24,16},{1,9},{9,1},{17,25},{25,17},{2,10},{10... | collective-permute-start | bytes 491528 | tf_op jit(solution)/shard_map/ppermute | solution.py:863
  11.4 4.1 %collective-permute-start.2 = (f32[16,640]{1,0:T(8,128)S(1)}, f32[16,640]{1,0:T(8,128)S(1)}, u32[]{:S(2)}, u32[]{:S(2)}) collective-permute-start(f32[16,640]{1,0:T(8,128)S(1)} %get-tuple-element.48.after), channel_id=1, source_target_pairs={{0,4},{4,0},{1,5},{5,1},{2,6},{6,2},{3,7},{7,3},{8,12},{12,8},{9,1... | collective-permute-start | bytes 122888 | tf_op jit(solution)/shard_map/ppermute | solution.py:863
  13.0 5.8 %collective-permute-start.6 = (f32[32,512]{1,0:T(8,128)S(1)}, f32[32,512]{1,0:T(8,128)S(1)}, u32[]{:S(2)}, u32[]{:S(2)}) collective-permute-start(f32[32,512]{1,0:T(8,128)S(1)} %get-tuple-element.62.refs_0_), channel_id=1, source_target_pairs={{0,16},{8,24},{16,0},{24,8},{1,17},{9,25},{17,1},{25,9},{2,18},{10... | collective-permute-start | bytes 196616 | tf_op jit(solution)/shard_map/ppermute | solution.py:863
  14.6 4.3 %collective-permute-start.7 = (f32[32,512]{1,0:T(8,128)S(1)}, f32[32,512]{1,0:T(8,128)S(1)}, u32[]{:S(2)}, u32[]{:S(2)}) collective-permute-start(f32[32,512]{1,0:T(8,128)S(1)} %get-tuple-element.63.refs_1_), channel_id=1, source_target_pairs={{0,16},{8,24},{16,0},{24,8},{1,17},{9,25},{17,1},{25,9},{2,18},{10... | collective-permute-start | bytes 196616 | tf_op jit(solution)/shard_map/ppermute | solution.py:863
  15.8 3.0 %collective-permute-start.5 = (f32[8,512]{1,0:T(8,128)S(1)}, f32[8,512]{1,0:T(8,128)S(1)}, u32[]{:S(2)}, u32[]{:S(2)}) collective-permute-start(f32[8,512]{1,0:T(8,128)S(1)} %pad_maximum_fusion.b.a), channel_id=1, source_target_pairs={{0,8},{8,0},{16,24},{24,16},{1,9},{9,1},{17,25},{25,17},{2,10},{10... | collective-permute-start | bytes 49160 | tf_op jit(solution)/shard_map/ppermute | solution.py:863
  15.9 4.9 %collective-permute-start.4 = (f32[24,512]{1,0:T(8,128)S(1)}, f32[24,512]{1,0:T(8,128)S(1)}, u32[]{:S(2)}, u32[]{:S(2)}) collective-permute-start(f32[24,512]{1,0:T(8,128)S(1)} %stacked.1.tail), channel_id=1, source_target_pairs={{0,16},{8,24},{16,0},{24,8},{1,17},{9,25},{17,1},{25,9},{2,18},{10... | collective-permute-start | bytes 147464 | tf_op jit(solution)/shard_map/ppermute | solution.py:863
  17.5 3.2 %collective-permute-start.9 = (f32[8,512]{1,0:T(8,128)S(1)}, f32[8,512]{1,0:T(8,128)S(1)}, u32[]{:S(2)}, u32[]{:S(2)}) collective-permute-start(f32[8,512]{1,0:T(8,128)S(1)} %pad_maximum_fusion.b.a), channel_id=1, source_target_pairs={{0,24},{8,16},{16,8},{24,0},{1,25},{9,17},{17,9},{25,1},{2,26},{10... | collective-permute-start | bytes 49160 | tf_op jit(solution)/shard_map/ppermute | solution.py:863
  18.9 1.9 %collective-permute-start.8 = (f32[16,512]{1,0:T(8,128)S(1)}, f32[16,512]{1,0:T(8,128)S(1)}, u32[]{:S(2)}, u32[]{:S(2)}) collective-permute-start(f32[16,512]{1,0:T(8,128)S(1)} %get-tuple-element.64.refs_0_), channel_id=1, source_target_pairs={{0,8},{8,0},{16,24},{24,16},{1,9},{9,1},{17,25},{25,17},{2,10},{10... | collective-permute-start | bytes 98312 | tf_op jit(solution)/shard_map/ppermute | solution.py:863
  19.3 2.4 %collective-permute-start.10 = (f32[16,512]{1,0:T(8,128)S(1)}, f32[16,512]{1,0:T(8,128)S(1)}, u32[]{:S(2)}, u32[]{:S(2)}) collective-permute-start(f32[16,512]{1,0:T(8,128)S(1)} %get-tuple-element.67.refs_1_), channel_id=1, source_target_pairs={{0,8},{8,0},{16,24},{24,16},{1,9},{9,1},{17,25},{25,17},{2,10},{10... | collective-permute-start | bytes 98312 | tf_op jit(solution)/shard_map/ppermute | solution.py:863
  19.5 2.1 %collective-permute-start.11 = (f32[16,512]{1,0:T(8,128)S(1)}, f32[16,512]{1,0:T(8,128)S(1)}, u32[]{:S(2)}, u32[]{:S(2)}) collective-permute-start(f32[16,512]{1,0:T(8,128)S(1)} %get-tuple-element.68.refs_2_), channel_id=1, source_target_pairs={{0,8},{8,0},{16,24},{24,16},{1,9},{9,1},{17,25},{25,17},{2,10},{10... | collective-permute-start | bytes 98312 | tf_op jit(solution)/shard_map/ppermute | solution.py:863
  20.6 1.2 %collective-permute-start.12 = (f32[16,512]{1,0:T(8,128)S(1)}, f32[16,512]{1,0:T(8,128)S(1)}, u32[]{:S(2)}, u32[]{:S(2)}) collective-permute-start(f32[16,512]{1,0:T(8,128)S(1)} %get-tuple-element.69.refs_3_), channel_id=1, source_target_pairs={{0,8},{8,0},{16,24},{24,16},{1,9},{9,1},{17,25},{25,17},{2,10},{10... | collective-permute-start | bytes 98312 | tf_op jit(solution)/shard_map/ppermute | solution.py:863

commit v3 on v2

--- a/solution.py
+++ b/solution.py
@@ -734,7 +734,7 @@
     first = pl.multiple_of(core * half, 8)
     var = jnp.concatenate([x[...] for x in mine] + [late[:8, :]], axis=0)
     fric[...] = half_rate(var, rims, turned, d, first, low, half)
-    size = 24
+    size = half
     last_v = {(c, p): jnp.where(low, vs_out[2 * c + p : 2 * c + p + 1, :], 0.0) for c, p in pairs(kdev)}
 
     def top(c, p, own):
@@ -791,13 +791,12 @@
         eta_own.at[:, :, pl.ds(skip, half - 8), :],
         eta_out.at[:, :, pl.ds(pl.multiple_of(own + skip, 8), half - 8), :],
     )
-    put(fric_own, fric_out.at[pl.ds(own, half), :])
     fric[pl.ds(own, half), :] = fric_own[...]
     fric[pl.ds(first, half), :] = half_rate(
         jnp.concatenate([x[...] for x in other] + [late[8:, :]], axis=0),
         rims[...], turned, d, first, jnp.logical_not(own_low), half,
     )
-    put(fric.at[pl.ds(first, half), :], fric_out.at[pl.ds(first, half), :])
+    put(fric, fric_out)
 
     r, rn = tile_rows(fric, half - 8, 8, half)
     r2 = r + rn
@@ -852,7 +851,7 @@
             pltpu.VMEM((kdev, 2, rows // 2, width), F32),
             pltpu.VMEM(d.shape, F32),
             pltpu.VMEM((kdev, 2, 8, width), F32),
-            pltpu.SemaphoreType.DMA((4 + rows // 2 // 24,)),
+            pltpu.SemaphoreType.DMA((3 + rows // 2 // 24,)),
         ],
         compiler_params=PARAMS,
         name="other_half",

time: 23.5 us -> 23.5 us (level)
  transfers between devices with their start and end apart: 13 -> 13, of which waited for: 5 -> 5; matrix products, arithmetic and copies ran while one was open for 0% -> 0% of each run, Pallas kernels for 18% -> 17%
where the time goes in v3:
time: 23.5 us; the launch traced here: 23.3 us
  starting transfers between devices  12.1 us (51%)
  Pallas kernels  7.65 us (33%)
  waiting for transfers between devices  2.56 us (11%)
  between operations  0.82 us (3%)
    ppermute x12, starting transfers between devices, swapped(): lax.ppermute(x, axis, [(i, i ^ bit) for i in range(lax.axis_size(axis))])  9.67 us
    ppermute x1, starting transfers between devices, body(): lax.ppermute(m2, 'tx', [(i, (i - 1 if i % 2 == 0 else i + 1) % ntx) for i...  2.47 us
    pallas_call x1, Pallas kernels, pack_columns(): pl.pallas_call(pack_columns_kernel, out_shape=(pltpu.VMEM((MSG, rows), F3...  2.01 us
    pallas_call x1, Pallas kernels, first_sweep(): pl.pallas_call(first_kernel, out_shape=(pltpu.VMEM(e.shape, F32), half, h...  1.94 us
    ppermute x12, waiting for transfers between devices, swapped(): lax.ppermute(x, axis, [(i, i ^ bit) for i in range(lax.axis_size(axis))])  1.57 us
    pallas_call x1, Pallas kernels, other_half(): pl.pallas_call(other_kernel, out_shape=(jax.ShapeDtypeStruct(du.shape, F3...  1.48 us
    ppermute x1, waiting for transfers between devices, body(): lax.ppermute(m2, 'tx', [(i, (i - 1 if i % 2 == 0 else i + 1) % ntx) for i...  0.99 us
    pallas_call x1, Pallas kernels, prepare(): pl.pallas_call(prepare_kernel, out_shape=(plane, plane, plane), in_specs=...  0.76 us
  transfers between devices with their start and end apart: 13, of which 5 were waited for; matrix products, arithmetic and copies ran while one was open for 0% of the time, Pallas kernels for 17%

profile of v3, /device:TPU:0, one launch (start us, length us, event | category | flops | bytes accessed | tf_op | source)
XLA Modules:
  0.0 23.3 jit_solution(876712487240803908)
XLA Ops:
  0.6 0.0 copy-start.2
  0.6 0.0 copy-start
  0.7 0.0 copy-start.3
  0.7 0.0 copy-start.1
  0.7 0.0 copy-start.4
  0.7 2.0 %pack_columns.1 = (f32[16,144]{1,0:T(8,128)S(1)}, f32[16,256]{1,0:T(8,128)S(1)}) custom-call(f32[2,2,144,512]{3,2,1,0:T(8,128)} %e.3, f32[2,2,144,512]{3,2,1,0:T(8,128)} %q.5, f32[144,512]{1,0:T(8,128)} %d.7, s32[144,512]{1,0:T(8,128)} %ints.1, f32[144,512]{1,0:T(8,128)} %r.3), custom_call_target="tpu_custom_call" | custom-call | tf_op jit(solution)/shard_map/pack_columns/pallas_call | solution.py:126
  2.7 3.1 %collective-permute-start.1 = (f32[16,256]{1,0:T(8,128)S(1)}, f32[16,256]{1,0:T(8,128)S(1)}, u32[]{:S(2)}, u32[]{:S(2)}) collective-permute-start(f32[16,256]{1,0:T(8,128)S(1)} %get-tuple-element.39.after.refs_1_), channel_id=1, source_target_pairs={{0,1},{1,0},{2,3},{3,2},{4,5},{5,4},{6,7},{7,6},{8,9},{9,8},{10,11... | collective-permute-start | bytes 49160 | tf_op jit(solution)/shard_map/ppermute | solution.py:862
  5.8 2.5 %collective-permute-start = (f32[16,144]{1,0:T(8,128)S(1)}, f32[16,144]{1,0:T(8,128)S(1)}, u32[]{:S(2)}, u32[]{:S(2)}) collective-permute-start(f32[16,144]{1,0:T(8,128)S(1)} %get-tuple-element.42.refs_0_), channel_id=1, source_target_pairs={{0,3},{1,2},{2,1},{3,0},{4,7},{5,6},{6,5},{7,4},{8,11},{9,10},{10,... | collective-permute-start | bytes 27656 | tf_op jit(solution)/shard_map/ppermute | solution.py:872
  8.3 0.0 copy-done.2
  8.3 0.0 copy-done
  8.3 0.0 copy-done.3
  8.3 0.0 copy-done.1
  8.3 0.0 copy-done.4
  8.3 0.1 pack.1
  8.4 1.9 %first_sweep.1 = (f32[2,2,144,512]{3,2,1,0:T(8,128)S(1)}, f32[80,512]{1,0:T(8,128)S(1)}, f32[80,512]{1,0:T(8,128)S(1)}, f32[2,144,512]{2,1,0:T(8,128)S(1)}) custom-call(f32[2,2,144,512]{3,2,1,0:T(8,128)S(1)} %copy-done.1, f32[2,2,144,512]{3,2,1,0:T(8,128)S(1)} %copy-done, f32[144,512]{1,0:T(8,128)S(1)} %copy-done.2, ...), custom_call_target="tpu_custom_call" | custom-call | flops 23592960 | bytes 47185920 | tf_op jit(solution)/shard_map/first_sweep/pallas_call | solution.py:257
  10.3 1.0 %collective-permute-done.f2.refs_2_ = f32[16,144]{1,0:T(8,128)S(1)} collective-permute-done((f32[16,144]{1,0:T(8,128)S(1)}, f32[16,144]{1,0:T(8,128)S(1)}, u32[]{:S(2)}, u32[]{:S(2)}) %collective-permute-start) | collective-permute-done | bytes 9248 | tf_op jit(solution)/shard_map/ppermute | solution.py:872
  11.3 0.0 collective-permute-done.1.f1.refs_3_
  11.3 0.1 merge.1
  11.4 0.0 collective-permute-start.3
  11.4 1.6 %collective-permute-start.2 = (f32[16,640]{1,0:T(8,128)S(1)}, f32[16,640]{1,0:T(8,128)S(1)}, u32[]{:S(2)}, u32[]{:S(2)}) collective-permute-start(f32[16,640]{1,0:T(8,128)S(1)} %get-tuple-element.48.after), channel_id=1, source_target_pairs={{0,4},{4,0},{1,5},{5,1},{2,6},{6,2},{3,7},{7,3},{8,12},{12,8},{9,1... | collective-permute-start | bytes 122888 | tf_op jit(solution)/shard_map/ppermute | solution.py:862
  13.0 0.0 collective-permute-done.3.a
  13.0 1.6 %collective-permute-start.6 = (f32[32,512]{1,0:T(8,128)S(1)}, f32[32,512]{1,0:T(8,128)S(1)}, u32[]{:S(2)}, u32[]{:S(2)}) collective-permute-start(f32[32,512]{1,0:T(8,128)S(1)} %get-tuple-element.62.refs_0_), channel_id=1, source_target_pairs={{0,16},{8,24},{16,0},{24,8},{1,17},{9,25},{17,1},{25,9},{2,18},{10... | collective-permute-start | bytes 196616 | tf_op jit(solution)/shard_map/ppermute | solution.py:862
  14.6 0.5 %collective-permute-start.7 = (f32[32,512]{1,0:T(8,128)S(1)}, f32[32,512]{1,0:T(8,128)S(1)}, u32[]{:S(2)}, u32[]{:S(2)}) collective-permute-start(f32[32,512]{1,0:T(8,128)S(1)} %get-tuple-element.63.refs_1_), channel_id=1, source_target_pairs={{0,16},{8,24},{16,0},{24,8},{1,17},{9,25},{17,1},{25,9},{2,18},{10... | collective-permute-start | bytes 196616 | tf_op jit(solution)/shard_map/ppermute | solution.py:862
  15.1 0.4 %collective-permute-done.2.refs_6_.refs_7_ = f32[16,640]{1,0:T(8,128)S(1)} collective-permute-done((f32[16,640]{1,0:T(8,128)S(1)}, f32[16,640]{1,0:T(8,128)S(1)}, u32[]{:S(2)}, u32[]{:S(2)}) %collective-permute-start.2) | collective-permute-done | bytes 40992 | tf_op jit(solution)/shard_map/ppermute | solution.py:862
  15.5 0.2 %rim.1 = (f32[4,512]{1,0:T(4,128)S(1)}, f32[4,512]{1,0:T(4,128)S(1)}) custom-call(f32[16,512]{1,0:T(8,128)S(1)} %get-tuple-element.59.after.a, f32[16,144]{1,0:T(8,128)S(1)} %get-tuple-element.42.refs_0_, f32[16,256]{1,0:T(8,128)S(1)} %get-tuple-element.39.after.refs_1_, f32[16,144]{1,0:T(8,128)S(1)} %collective-permute-done.f2.refs_2_, ...), custom_call_target="tpu_custom_call" | custom-call | tf_op jit(solution)/shard_map/rim/pallas_call | solution.py:547
  15.8 0.1 collective-permute-start.5
  15.9 1.6 %collective-permute-start.4 = (f32[24,512]{1,0:T(8,128)S(1)}, f32[24,512]{1,0:T(8,128)S(1)}, u32[]{:S(2)}, u32[]{:S(2)}) collective-permute-start(f32[24,512]{1,0:T(8,128)S(1)} %stacked.1.tail), channel_id=1, source_target_pairs={{0,16},{8,24},{16,0},{24,8},{1,17},{9,25},{17,1},{25,9},{2,18},{10... | collective-permute-start | bytes 147464 | tf_op jit(solution)/shard_map/ppermute | solution.py:862
  17.5 0.3 %collective-permute-start.9 = (f32[8,512]{1,0:T(8,128)S(1)}, f32[8,512]{1,0:T(8,128)S(1)}, u32[]{:S(2)}, u32[]{:S(2)}) collective-permute-start(f32[8,512]{1,0:T(8,128)S(1)} %pad_maximum_fusion.b.a), channel_id=1, source_target_pairs={{0,24},{8,16},{16,8},{24,0},{1,25},{9,17},{17,9},{25,1},{2,26},{10... | collective-permute-start | bytes 49160 | tf_op jit(solution)/shard_map/ppermute | solution.py:862
  17.7 0.3 %held_strips.1 = (f32[48,640]{1,0:T(8,128)S(1)}, f32[48,640]{1,0:T(8,128)S(1)}, f32[48,256]{1,0:T(8,128)S(1)}, f32[48,256]{1,0:T(8,128)S(1)}) custom-call(f32[16,144]{1,0:T(8,128)S(1)} %get-tuple-element.42.refs_0_, f32[16,256]{1,0:T(8,128)S(1)} %get-tuple-element.39.after.refs_1_, f32[16,144]{1,0:T(8,128)S(1)} %collective-permute-done.f2.refs_2_, ...), custom_call_target="tpu_custom_call" | custom-call | tf_op jit(solution)/shard_map/held_strips/pallas_call | solution.py:576
  18.0 0.8 %prepare.1 = (f32[2,2,144,512]{3,2,1,0:T(8,128)S(1)}, f32[2,2,144,512]{3,2,1,0:T(8,128)S(1)}, f32[2,2,144,512]{3,2,1,0:T(8,128)S(1)}) custom-call(f32[2,2,144,512]{3,2,1,0:T(8,128)S(1)} %get-tuple-element.41.e1_in, f32[2,2,144,512]{3,2,1,0:T(8,128)S(1)} %copy-done, f32[144,512]{1,0:T(8,128)S(1)} %get-tuple-element.40.mask.m, ...), custom_call_target="tpu_custom_call" | custom-call | flops 11796480 | bytes 47185920 | tf_op jit(solution)/shard_map/prepare/pallas_call | solution.py:627
  18.8 0.0 collective-permute-done.5.b
  18.8 0.0 collective-permute-done.6.refs_2_
  18.8 0.1 collective-permute-done.7.refs_3_
  18.9 0.3 %collective-permute-start.8 = (f32[16,512]{1,0:T(8,128)S(1)}, f32[16,512]{1,0:T(8,128)S(1)}, u32[]{:S(2)}, u32[]{:S(2)}) collective-permute-start(f32[16,512]{1,0:T(8,128)S(1)} %get-tuple-element.64.refs_0_), channel_id=1, source_target_pairs={{0,8},{8,0},{16,24},{24,16},{1,9},{9,1},{17,25},{25,17},{2,10},{10... | collective-permute-start | bytes 98312 | tf_op jit(solution)/shard_map/ppermute | solution.py:862
  19.3 0.2 %collective-permute-start.10 = (f32[16,512]{1,0:T(8,128)S(1)}, f32[16,512]{1,0:T(8,128)S(1)}, u32[]{:S(2)}, u32[]{:S(2)}) collective-permute-start(f32[16,512]{1,0:T(8,128)S(1)} %get-tuple-element.67.refs_1_), channel_id=1, source_target_pairs={{0,8},{8,0},{16,24},{24,16},{1,9},{9,1},{17,25},{25,17},{2,10},{10... | collective-permute-start | bytes 98312 | tf_op jit(solution)/shard_map/ppermute | solution.py:862
  19.5 0.3 %collective-permute-start.11 = (f32[16,512]{1,0:T(8,128)S(1)}, f32[16,512]{1,0:T(8,128)S(1)}, u32[]{:S(2)}, u32[]{:S(2)}) collective-permute-start(f32[16,512]{1,0:T(8,128)S(1)} %get-tuple-element.68.refs_2_), channel_id=1, source_target_pairs={{0,8},{8,0},{16,24},{24,16},{1,9},{9,1},{17,25},{25,17},{2,10},{10... | collective-permute-start | bytes 98312 | tf_op jit(solution)/shard_map/ppermute | solution.py:862
  19.8 0.9 %collective-permute-done.9.refs_0_ = f32[8,512]{1,0:T(8,128)S(1)} collective-permute-done((f32[8,512]{1,0:T(8,128)S(1)}, f32[8,512]{1,0:T(8,128)S(1)}, u32[]{:S(2)}, u32[]{:S(2)}) %collective-permute-start.9) | collective-permute-done | bytes 16416 | tf_op jit(solution)/shard_map/ppermute | solution.py:862
  20.6 0.2 collective-permute-start.12
  20.8 0.0 collective-permute-done.4.partner
  20.8 0.0 collective-permute-done.8.after.refs_0_
  20.8 0.7 %own_half.1 = (f32[2,2,72,512]{3,2,1,0:T(8,128)S(1)}, f32[2,2,72,512]{3,2,1,0:T(8,128)S(1)}, f32[72,512]{1,0:T(8,128)S(1)}, f32[8,512]{1,0:T(8,128)S(1)}, f32[8,512]{1,0:T(8,128)S(1)}, /*index=5*/f32[256,128]{1,0:T(8,128)S(1)}) custom-call(f32[2,2,144,512]{3,2,1,0:T(8,128)S(1)} %get-tuple-element.53.du, f32[2,2,144,512]{3,2,1,0:T(8,128)S(1)} %get-tuple-element.54.dv, ...), custom_call_target="tpu_custom_call" | custom-call | tf_op jit(solution)/shard_map/own_half/pallas_call | solution.py:757
  21.5 0.1 sub.3.eta_own
  21.6 0.0 collective-permute-done.10.refs_1_
  21.6 0.0 collective-permute-done.11.refs_2_
  21.6 0.2 collective-permute-done.12.refs_3_
  21.8 1.5 %other_half.1 = (f32[2,2,144,512]{3,2,1,0:T(8,128)}, f32[144,512]{1,0:T(8,128)}) custom-call(f32[2,2,144,512]{3,2,1,0:T(8,128)S(1)} %get-tuple-element.53.du, f32[2,2,144,512]{3,2,1,0:T(8,128)S(1)} %get-tuple-element.54.dv, f32[2,2,144,512]{3,2,1,0:T(8,128)S(1)} %get-tuple-element.55.refs_0_.base, f32[2,144,512]{2,1,0:T(8,128)S(1)} %get-tuple-element.56.coef, ...), custom_call_target="tpu_custom_call" | custom-call | tf_op jit(solution)/shard_map/other_half/pallas_call | solution.py:845
  (6 shorter events, 0.1 us)
Async XLA Ops:
  0.6 7.6 %copy-start.2 = (f32[144,512]{1,0:T(8,128)S(1)}, f32[144,512]{1,0:T(8,128)}, u32[]{:S(2)}) copy-start(f32[144,512]{1,0:T(8,128)} %d.7) | copy-start | bytes 884740
  0.6 7.6 %copy-start = (f32[2,2,144,512]{3,2,1,0:T(8,128)S(1)}, f32[2,2,144,512]{3,2,1,0:T(8,128)}, u32[]{:S(2)}) copy-start(f32[2,2,144,512]{3,2,1,0:T(8,128)} %q.5) | copy-start | bytes 3538948
  0.7 7.6 %copy-start.3 = (f32[144,512]{1,0:T(8,128)S(1)}, f32[144,512]{1,0:T(8,128)}, u32[]{:S(2)}) copy-start(f32[144,512]{1,0:T(8,128)} %r.3) | copy-start | bytes 884740
  0.7 7.6 %copy-start.1 = (f32[2,2,144,512]{3,2,1,0:T(8,128)S(1)}, f32[2,2,144,512]{3,2,1,0:T(8,128)}, u32[]{:S(2)}) copy-start(f32[2,2,144,512]{3,2,1,0:T(8,128)} %e.3) | copy-start | bytes 3538948
  0.7 7.6 %copy-start.4 = (s32[144,512]{1,0:T(8,128)S(1)}, s32[144,512]{1,0:T(8,128)}, u32[]{:S(2)}) copy-start(s32[144,512]{1,0:T(8,128)} %ints.1) | copy-start | bytes 884740
  2.7 8.6 %collective-permute-start.1 = (f32[16,256]{1,0:T(8,128)S(1)}, f32[16,256]{1,0:T(8,128)S(1)}, u32[]{:S(2)}, u32[]{:S(2)}) collective-permute-start(f32[16,256]{1,0:T(8,128)S(1)} %get-tuple-element.39.after.refs_1_), channel_id=1, source_target_pairs={{0,1},{1,0},{2,3},{3,2},{4,5},{5,4},{6,7},{7,6},{8,9},{9,8},{10,11... | collective-permute-start | bytes 49160 | tf_op jit(solution)/shard_map/ppermute | solution.py:862
  5.8 5.5 %collective-permute-start = (f32[16,144]{1,0:T(8,128)S(1)}, f32[16,144]{1,0:T(8,128)S(1)}, u32[]{:S(2)}, u32[]{:S(2)}) collective-permute-start(f32[16,144]{1,0:T(8,128)S(1)} %get-tuple-element.42.refs_0_), channel_id=1, source_target_pairs={{0,3},{1,2},{2,1},{3,0},{4,7},{5,6},{6,5},{7,4},{8,11},{9,10},{10,... | collective-permute-start | bytes 27656 | tf_op jit(solution)/shard_map/ppermute | solution.py:872
  11.4 1.6 %collective-permute-start.3 = (f32[80,512]{1,0:T(8,128)S(1)}, f32[80,512]{1,0:T(8,128)S(1)}, u32[]{:S(2)}, u32[]{:S(2)}) collective-permute-start(f32[80,512]{1,0:T(8,128)S(1)} %get-tuple-element.57), channel_id=1, source_target_pairs={{0,8},{8,0},{16,24},{24,16},{1,9},{9,1},{17,25},{25,17},{2,10},{10... | collective-permute-start | bytes 491528 | tf_op jit(solution)/shard_map/ppermute | solution.py:862
  11.4 4.1 %collective-permute-start.2 = (f32[16,640]{1,0:T(8,128)S(1)}, f32[16,640]{1,0:T(8,128)S(1)}, u32[]{:S(2)}, u32[]{:S(2)}) collective-permute-start(f32[16,640]{1,0:T(8,128)S(1)} %get-tuple-element.48.after), channel_id=1, source_target_pairs={{0,4},{4,0},{1,5},{5,1},{2,6},{6,2},{3,7},{7,3},{8,12},{12,8},{9,1... | collective-permute-start | bytes 122888 | tf_op jit(solution)/shard_map/ppermute | solution.py:862
  13.0 5.8 %collective-permute-start.6 = (f32[32,512]{1,0:T(8,128)S(1)}, f32[32,512]{1,0:T(8,128)S(1)}, u32[]{:S(2)}, u32[]{:S(2)}) collective-permute-start(f32[32,512]{1,0:T(8,128)S(1)} %get-tuple-element.62.refs_0_), channel_id=1, source_target_pairs={{0,16},{8,24},{16,0},{24,8},{1,17},{9,25},{17,1},{25,9},{2,18},{10... | collective-permute-start | bytes 196616 | tf_op jit(solution)/shard_map/ppermute | solution.py:862
  14.6 4.3 %collective-permute-start.7 = (f32[32,512]{1,0:T(8,128)S(1)}, f32[32,512]{1,0:T(8,128)S(1)}, u32[]{:S(2)}, u32[]{:S(2)}) collective-permute-start(f32[32,512]{1,0:T(8,128)S(1)} %get-tuple-element.63.refs_1_), channel_id=1, source_target_pairs={{0,16},{8,24},{16,0},{24,8},{1,17},{9,25},{17,1},{25,9},{2,18},{10... | collective-permute-start | bytes 196616 | tf_op jit(solution)/shard_map/ppermute | solution.py:862
  15.8 3.0 %collective-permute-start.5 = (f32[8,512]{1,0:T(8,128)S(1)}, f32[8,512]{1,0:T(8,128)S(1)}, u32[]{:S(2)}, u32[]{:S(2)}) collective-permute-start(f32[8,512]{1,0:T(8,128)S(1)} %pad_maximum_fusion.b.a), channel_id=1, source_target_pairs={{0,8},{8,0},{16,24},{24,16},{1,9},{9,1},{17,25},{25,17},{2,10},{10... | collective-permute-start | bytes 49160 | tf_op jit(solution)/shard_map/ppermute | solution.py:862
  15.9 4.9 %collective-permute-start.4 = (f32[24,512]{1,0:T(8,128)S(1)}, f32[24,512]{1,0:T(8,128)S(1)}, u32[]{:S(2)}, u32[]{:S(2)}) collective-permute-start(f32[24,512]{1,0:T(8,128)S(1)} %stacked.1.tail), channel_id=1, source_target_pairs={{0,16},{8,24},{16,0},{24,8},{1,17},{9,25},{17,1},{25,9},{2,18},{10... | collective-permute-start | bytes 147464 | tf_op jit(solution)/shard_map/ppermute | solution.py:862
  17.5 3.2 %collective-permute-start.9 = (f32[8,512]{1,0:T(8,128)S(1)}, f32[8,512]{1,0:T(8,128)S(1)}, u32[]{:S(2)}, u32[]{:S(2)}) collective-permute-start(f32[8,512]{1,0:T(8,128)S(1)} %pad_maximum_fusion.b.a), channel_id=1, source_target_pairs={{0,24},{8,16},{16,8},{24,0},{1,25},{9,17},{17,9},{25,1},{2,26},{10... | collective-permute-start | bytes 49160 | tf_op jit(solution)/shard_map/ppermute | solution.py:862
  18.9 1.9 %collective-permute-start.8 = (f32[16,512]{1,0:T(8,128)S(1)}, f32[16,512]{1,0:T(8,128)S(1)}, u32[]{:S(2)}, u32[]{:S(2)}) collective-permute-start(f32[16,512]{1,0:T(8,128)S(1)} %get-tuple-element.64.refs_0_), channel_id=1, source_target_pairs={{0,8},{8,0},{16,24},{24,16},{1,9},{9,1},{17,25},{25,17},{2,10},{10... | collective-permute-start | bytes 98312 | tf_op jit(solution)/shard_map/ppermute | solution.py:862
  19.3 2.4 %collective-permute-start.10 = (f32[16,512]{1,0:T(8,128)S(1)}, f32[16,512]{1,0:T(8,128)S(1)}, u32[]{:S(2)}, u32[]{:S(2)}) collective-permute-start(f32[16,512]{1,0:T(8,128)S(1)} %get-tuple-element.67.refs_1_), channel_id=1, source_target_pairs={{0,8},{8,0},{16,24},{24,16},{1,9},{9,1},{17,25},{25,17},{2,10},{10... | collective-permute-start | bytes 98312 | tf_op jit(solution)/shard_map/ppermute | solution.py:862
  19.5 2.1 %collective-permute-start.11 = (f32[16,512]{1,0:T(8,128)S(1)}, f32[16,512]{1,0:T(8,128)S(1)}, u32[]{:S(2)}, u32[]{:S(2)}) collective-permute-start(f32[16,512]{1,0:T(8,128)S(1)} %get-tuple-element.68.refs_2_), channel_id=1, source_target_pairs={{0,8},{8,0},{16,24},{24,16},{1,9},{9,1},{17,25},{25,17},{2,10},{10... | collective-permute-start | bytes 98312 | tf_op jit(solution)/shard_map/ppermute | solution.py:862
  20.6 1.2 %collective-permute-start.12 = (f32[16,512]{1,0:T(8,128)S(1)}, f32[16,512]{1,0:T(8,128)S(1)}, u32[]{:S(2)}, u32[]{:S(2)}) collective-permute-start(f32[16,512]{1,0:T(8,128)S(1)} %get-tuple-element.69.refs_3_), channel_id=1, source_target_pairs={{0,8},{8,0},{16,24},{24,16},{1,9},{9,1},{17,25},{25,17},{2,10},{10... | collective-permute-start | bytes 98312 | tf_op jit(solution)/shard_map/ppermute | solution.py:862
